TPU v7x, 128 devices: a whole 4x4x4 slice. The times are simulated.
128 devices in a mesh: users: 32 (over z, x, core), items: 4 (over y).
Axes of the slice: x: 4, y: 4, z: 4, core: 2. Of those that a mesh axis runs over, the one named last changes fastest.
Arguments:
- user_old: float32 [32768, 128], P(('users', 'items')), may hold values from -3 to 3
- item_old: float32 [65536, 128], P(('users', 'items'))
- item_rhs: float32 [65536, 128], P(('users', 'items')), may hold values from -360 to 360
- user_gram: float32 [128, 128], replicated
- req_count: int32 [128, 128], P(('users', 'items')), may hold values from 1 to 16, as said below
- req_item: int32 [128, 128, 16], P(('users', 'items')), may hold values from 0 to 511
- req_user: int32 [128, 128, 16], P(('users', 'items')), may hold values from 0 to 255
- weight: float32 [128, 128, 16], P(('users', 'items')), may hold values from 1 to 20
- rating: float32 [128, 128, 16], P(('users', 'items')), may hold values from -4 to 4
Outputs:
- user_new: float32 [32768, 128], P(('users', 'items'))
- item_new: float32 [65536, 128], P(('users', 'items'))
Inputs may be any that keep to these rules, and one draw needn't show every extreme that they name: In every draw some item owner receives 16 live slots from every device; every other count lies between 1 and 16. Only the first req_count[d, o] slots of a pair carry a rating.
All inputs are finite; a program needn't handle non-finite values.
Results may differ from a plain program's by a relative error of at most 0.0003.
Values sent between devices are 32-bit elements; how exact they have to be, the bound alone decides.
A program may use at most 64 MiB of HBM per device.

v0:
```python
import jax
import jax.numpy as jnp
from jax import lax
from jax.sharding import PartitionSpec as P

ITERS = 8


ridge = 1.0
highest = lax.Precision.HIGHEST


def slot_terms(weight, rating, counts):
    slot_index = jnp.arange(weight.shape[-1], dtype=jnp.int32)
    live = slot_index < counts[..., None]
    weights = jnp.where(live, weight, 0.0)
    coefs = jnp.where(live, (1.0 + weight) * rating, 0.0)
    return (weights, coefs)


def one_hot_table(targets, groups):
    return (targets[:, None] == jnp.arange(groups, dtype=jnp.int32)[None, :]).astype(jnp.float32)


def pick_rows(table, source):
    return jnp.dot(table, source, precision=highest)


def fold_rows(table, terms):
    return lax.dot_general(table, terms, (((0,), (0,)), ((), ())), precision=highest)


def refine(start, base, rows, targets, weights, coefs, gram):
    groups = start.shape[0]
    shifted = gram + ridge * jnp.eye(gram.shape[0], dtype=gram.dtype)
    table = one_hot_table(targets, groups)

    def operate(vector):
        along = jnp.sum(rows * pick_rows(table, vector), axis=1) * weights
        local_part = jnp.dot(vector, shifted, precision=highest)
        return local_part + fold_rows(table, along[:, None] * rows)

    right = base + fold_rows(table, coefs[:, None] * rows)
    resid = right - operate(start)
    direction = resid
    squares = jnp.sum(resid * resid, axis=1)
    solution = start
    for iteration in range(ITERS):
        image = operate(direction)
        alpha = squares / jnp.sum(direction * image, axis=1)
        solution = solution + alpha[:, None] * direction
        resid = resid - alpha[:, None] * image
        fresh = jnp.sum(resid * resid, axis=1)
        direction = resid + (fresh / squares)[:, None] * direction
        squares = fresh
    return solution


def per_device(
    user_old, item_old, item_rhs, user_gram, req_count, req_item, req_user, weight, rating
):
    senders = lax.axis_size(("users", "items"))
    capacity = req_item.shape[2]
    rank = item_old.shape[1]
    weights, coefs = slot_terms(weight[0], rating[0], req_count[0])
    item_gram = lax.psum(jnp.dot(item_old.T, item_old, precision=highest), ("users", "items"))
    asked = lax.all_to_all(req_item[0], ("users", "items"), split_axis=0, concat_axis=0, tiled=True)
    asked_flat = asked.reshape(-1)
    found = pick_rows(one_hot_table(asked_flat, item_old.shape[0]), item_old).reshape(
        senders, capacity, rank
    )
    fetched = lax.all_to_all(found, ("users", "items"), split_axis=0, concat_axis=0, tiled=True)
    fetched = fetched.reshape(senders * capacity, rank)
    members = req_user[0].reshape(-1)
    user_new = refine(
        user_old, 0.0, fetched, members, weights.reshape(-1), coefs.reshape(-1), item_gram
    )
    user_total = user_gram + lax.psum(
        jnp.dot(user_new.T, user_new, precision=highest), ("users", "items")
    )
    outgoing = pick_rows(one_hot_table(members, user_new.shape[0]), user_new).reshape(
        senders, capacity, rank
    )
    factors = jnp.stack([weights, coefs], axis=-1)
    arrived, arrived_terms = (
        lax.all_to_all(outgoing, ("users", "items"), split_axis=0, concat_axis=0, tiled=True),
        lax.all_to_all(factors, ("users", "items"), split_axis=0, concat_axis=0, tiled=True),
    )
    arrived = arrived.reshape(senders * capacity, rank)
    arrived_terms = arrived_terms.reshape(senders * capacity, 2)
    item_new = refine(
        item_old,
        item_rhs,
        arrived,
        asked_flat,
        arrived_terms[:, 0],
        arrived_terms[:, 1],
        user_total,
    )
    return (user_new, item_new)


def solution(mesh):
    in_specs = (
        P(("users", "items"), None),
        P(("users", "items"), None),
        P(("users", "items"), None),
        P(),
        P(("users", "items"), None),
        P(("users", "items"), None, None),
        P(("users", "items"), None, None),
        P(("users", "items"), None, None),
        P(("users", "items"), None, None),
    )
    out_specs = (P(("users", "items"), None), P(("users", "items"), None))
    return jax.shard_map(
        per_device, mesh=mesh, in_specs=in_specs, out_specs=out_specs, check_vma=False
    )
```

profile of v0, /device:TPU:1, one launch (start us, length us, event | category | flops | bytes accessed | tf_op | source)
XLA Modules:
  0.0 425.5 jit_solution(7136742951567536876)
XLA Ops:
  7.2 0.8 copy.95
  8.0 20.9 %all_to_all.24 = s32[128,1,16]{2,1,0:T(1,128)S(1)} all-to-all(s32[128,1,16]{2,1,0:T(1,128)S(1)} %bitcast.136), channel_id=1, replica_groups=mesh['users'=32,'items'=4] {'users','items'}, dimensions={0} | all-to-all | bytes 16384 | tf_op jit(solution)/shard_map/all_to_all | solution.py:67
  28.9 0.5 broadcast.106
  29.4 0.8 reduce.3
  30.3 3.9 fusion.18
  34.3 4.3 %all-to-all-start.1 = ((f32[128,16,128]{2,1,0:T(8,128)}), f32[128,16,128]{2,1,0:T(8,128)S(1)}, u32[]{:S(2)}, u32[]{:S(2)}) async-start(f32[128,16,128]{2,1,0:T(8,128)} %bitcast.2), calls=%async_computation.1 | async-start | bytes 2097152 | tf_op jit(solution)/shard_map/all_to_all | solution.py:72
  38.7 1.2 fusion.134
  40.8 0.8 copy.106
  41.6 16.6 %all-to-all-done.1 = f32[128,16,128]{2,1,0:T(8,128)S(1)} async-done(((f32[128,16,128]{2,1,0:T(8,128)}), f32[128,16,128]{2,1,0:T(8,128)S(1)}, u32[]{:S(2)}, u32[]{:S(2)}) %all-to-all-start.1) | async-done | bytes 1048608 | tf_op jit(solution)/shard_map/all_to_all | solution.py:72
  58.1 4.1 all-to-all-start.2
  62.6 1.6 fusion.65
  64.2 1.6 fusion.55
  65.8 1.6 fusion.56
  67.4 117.0 %all-reduce.3.cloned.1.call-done = f32[128,128]{1,0:T(8,128)} async-done(((f32[128,128]{1,0:T(8,128)}), f32[128,128]{1,0:T(8,128)}) %all-reduce.3.cloned.1.call-update) | async-done | bytes 65552 | tf_op jit(solution)/shard_map/psum | solution.py:66
  184.4 1.2 fusion.81
  185.6 1.5 fusion.66
  187.2 1.6 fusion.54
  189.2 1.5 fusion.67
  190.8 1.6 fusion.53
  192.9 1.5 fusion.68
  194.4 1.6 fusion.52
  196.5 1.7 fusion.69
  198.2 1.6 fusion.51
  200.3 1.5 fusion.70
  201.9 1.6 fusion.50
  203.9 1.5 fusion.71
  205.5 1.6 fusion.49
  207.5 1.5 fusion.72
  209.1 1.6 fusion.48
  211.2 1.9 fusion.73
  213.1 1.6 fusion.47
  215.2 2.1 fusion.46
  217.3 5.1 %all-to-all-start.3 = ((f32[128,16,128]{2,1,0:T(8,128)}), f32[128,16,128]{2,1,0:T(8,128)S(1)}, u32[]{:S(2)}, u32[]{:S(2)}) async-start(f32[128,16,128]{2,1,0:T(8,128)} %bitcast.8), calls=%async_computation.3 | async-start | bytes 2097152 | tf_op jit(solution)/shard_map/all_to_all | solution.py:86
  222.5 0.9 fusion.135
  223.8 0.8 copy.118
  224.6 144.1 %all-reduce.5.cloned.1.call-done = f32[128,128]{1,0:T(8,128)} async-done(((f32[128,128]{1,0:T(8,128)}), f32[128,128]{1,0:T(8,128)}) %all-reduce.5.cloned.1.call-update) | async-done | bytes 65552 | tf_op jit(solution)/shard_map/psum | solution.py:78
  368.6 0.9 convert_add_fusion
  369.9 1.6 fusion.83
  371.5 0.6 bitcast_multiply_fusion.8
  372.2 1.8 fusion.75
  374.0 1.8 fusion.77
  375.8 2.5 fusion.64
  378.7 1.8 fusion.14
  380.5 0.4 multiply_reduce_fusion.13
  381.1 2.3 fusion.63
  383.8 1.8 fusion.12
  386.2 2.3 fusion.62
  388.9 1.8 fusion.10
  390.8 0.4 multiply_reduce_fusion.9
  391.3 2.5 fusion.61
  394.2 1.8 fusion.8
  396.1 0.4 multiply_reduce_fusion.7
  396.7 2.3 fusion.60
  399.3 1.8 fusion.6
  401.2 0.4 multiply_reduce_fusion.5
  401.8 2.3 fusion.59
  404.4 1.8 fusion.4
  406.3 0.4 multiply_reduce_fusion.3
  406.9 2.6 fusion.58
  409.8 1.8 fusion.2
  411.6 0.4 multiply_reduce_fusion.1
  412.3 2.3 fusion.57
  414.9 1.8 fusion
  417.5 0.8 copy.119
  (138 shorter events, 10.6 us)
Async XLA Ops:
  34.2 4.4 %copy-start.1 = (f32[512,128]{1,0:T(8,128)S(1)}, f32[512,128]{1,0:T(8,128)}, u32[]{:S(2)}) copy-start(f32[512,128]{1,0:T(8,128)} %param.10) | copy-start | bytes 786436
  34.2 5.7 %copy-start.7 = (s32[1,128,16]{1,2,0:T(8,128)S(1)}, s32[1,128,16]{1,2,0:T(8,128)}, u32[]{:S(2)}) copy-start(s32[1,128,16]{1,2,0:T(8,128)} %param.15) | copy-start | bytes 24580
  34.2 5.9 %copy-start.8 = (s32[1,128]{1,0:T(1,128)S(1)}, s32[1,128]{1,0:T(1,128)}, u32[]{:S(2)}) copy-start(s32[1,128]{1,0:T(1,128)} %param.13) | copy-start | bytes 1540
  34.2 6.0 %copy-start.5 = (f32[1,128,16]{1,2,0:T(8,128)S(1)}, f32[1,128,16]{1,2,0:T(8,128)}, u32[]{:S(2)}) copy-start(f32[1,128,16]{1,2,0:T(8,128)} %param.16) | copy-start | bytes 24580
  34.3 6.2 %copy-start.6 = (f32[1,128,16]{1,2,0:T(8,128)S(1)}, f32[1,128,16]{1,2,0:T(8,128)}, u32[]{:S(2)}) copy-start(f32[1,128,16]{1,2,0:T(8,128)} %param.17) | copy-start | bytes 24580
  34.3 23.9 %all-to-all-start.1 = ((f32[128,16,128]{2,1,0:T(8,128)}), f32[128,16,128]{2,1,0:T(8,128)S(1)}, u32[]{:S(2)}, u32[]{:S(2)}) async-start(f32[128,16,128]{2,1,0:T(8,128)} %bitcast.2), calls=%async_computation.1 | async-start | bytes 2097152 | tf_op jit(solution)/shard_map/all_to_all | solution.py:72
  38.6 2.1 copy-start.2
  38.6 145.8 %all-reduce.3.cloned.1.call-start = ((), (), s32[]{:S(2)}) async-start(), calls=%async_computation.4 | async-start | bytes 131072 | tf_op jit(solution)/shard_map/psum | solution.py:66
  58.1 159.2 %all-to-all-start.2 = ((f32[128,16,2]{1,2,0:T(2,128)}), f32[128,16,2]{1,2,0:T(2,128)S(1)}, u32[]{:S(2)}, u32[]{:S(2)}) async-start(f32[128,16,2]{1,2,0:T(2,128)} %copy.106), calls=%async_computation.2 | async-start | bytes 262144 | tf_op jit(solution)/shard_map/all_to_all | solution.py:87
  185.6 3.2 copy-start
  217.3 6.2 %copy-start.3 = (f32[512,128]{1,0:T(8,128)S(1)}, f32[512,128]{1,0:T(8,128)}, u32[]{:S(2)}) copy-start(f32[512,128]{1,0:T(8,128)} %param.11) | copy-start | bytes 786436
  217.3 152.6 %all-to-all-start.3 = ((f32[128,16,128]{2,1,0:T(8,128)}), f32[128,16,128]{2,1,0:T(8,128)S(1)}, u32[]{:S(2)}, u32[]{:S(2)}) async-start(f32[128,16,128]{2,1,0:T(8,128)} %bitcast.8), calls=%async_computation.3 | async-start | bytes 2097152 | tf_op jit(solution)/shard_map/all_to_all | solution.py:86
  222.4 146.2 %copy-start.4 = (f32[128,128]{1,0:T(8,128)S(1)}, f32[128,128]{1,0:T(8,128)}, u32[]{:S(2)}) copy-start(f32[128,128]{1,0:T(8,128)} %param.12) | copy-start | bytes 196612
  222.4 146.2 %all-reduce.5.cloned.1.call-start = ((), (), s32[]{:S(2)}) async-start(), calls=%async_computation.5 | async-start | bytes 131072 | tf_op jit(solution)/shard_map/psum | solution.py:78
Sparse Core Ops, SparseCore 0:
  44.8 139.6 all-reduce.2
  229.3 139.2 all-reduce.4
where the time goes:
time: 430 us; the launch traced here: 425 us
  waiting for transfers between devices  278 us (65%)
  matrix products  84 us (20%)
  blocking collectives  20.9 us (5%)
  between operations  15.3 us (4%)
  starting transfers between devices  13.6 us (3%)
  other arithmetic  8.73 us (2%)
  local copies, waits for them, and re-layouts  5.23 us (1%)
    psum x1, waiting for transfers between devices, per_device(): lax.psum(jnp.dot(user_new.T, user_new, precision=highest), ('users', 'ite...  144 us
    psum x1, waiting for transfers between devices, per_device(): lax.psum(jnp.dot(item_old.T, item_old, precision=highest), ('users', 'ite...  117 us
    dot_general x19, matrix products, pick_rows(): return jnp.dot(table, source, precision=highest)  39.7 us
    dot_general x20, matrix products, fold_rows(): lax.dot_general(table, terms, (((0,), (0,)), ((), ())), precision=highest)  34.3 us
    all_to_all x1, blocking collectives, per_device(): lax.all_to_all(req_item[0], ('users', 'items'), split_axis=0, concat_axis...  20.9 us
    all_to_all x1, waiting for transfers between devices, per_device(): lax.all_to_all(found, ('users', 'items'), split_axis=0, concat_axis=0, ti...  16.6 us
  transfers between devices with their start and end apart: 5, of which 3 were waited for; matrix products, arithmetic and copies ran while one was open for 10% of the time, Pallas kernels for 0%

commit v1 on v0

v1 whole, which is shorter than its diff:
```python
import functools
import jax
import jax.numpy as jnp
from jax import lax
from jax.sharding import PartitionSpec as P
from jax.experimental import pallas as pl
from jax.experimental.pallas import tpu as pltpu

ITERS = 8
RIDGE = 1.0
CHUNK = 512
MESH = pl.DeviceIdType.MESH
F32 = jnp.float32
BF16 = jnp.bfloat16


def split2(value):
    high = value.astype(BF16)
    return high, (value - high.astype(F32)).astype(BF16)


def split3(value):
    high = value.astype(BF16)
    rest = value - high.astype(F32)
    middle = rest.astype(BF16)
    return high, middle, (rest - middle.astype(F32)).astype(BF16)


def dot(left, right):
    return jnp.dot(left, right, preferred_element_type=F32)


def halves(value):
    width = value.shape[1] // 2
    return value[:, :width] + value[:, width:]


def iota(shape, axis):
    return lax.broadcasted_iota(jnp.int32, shape, axis)


def owner_table(first, rows, capacity, senders):
    owner = lax.div(iota((rows, senders), 0), capacity) + first // capacity
    return (owner == iota((rows, senders), 1)).astype(F32).astype(BF16)


def spread(pieces, first, rows, capacity, senders):
    table = owner_table(first, rows, capacity, senders)
    wide = halves(dot(table, jnp.concatenate(pieces[:2], axis=1)))
    if len(pieces) > 2:
        wide = wide + dot(table, pieces[2])
    return wide


def column(wide, which, capacity):
    slot = lax.rem(iota(wide.shape, 0), capacity) + which * capacity
    return jnp.sum(jnp.where(slot == iota(wide.shape, 1), wide, 0.0), axis=1, keepdims=True)


def row_table(indices, groups, capacity, out):
    senders = indices.shape[1]
    both = jnp.concatenate(split2(indices), axis=0)
    slots = senders * capacity
    for first in range(0, slots, CHUNK):
        owner = lax.div(iota((senders, CHUNK), 1), capacity) + first // capacity
        table = (owner == iota((senders, CHUNK), 0)).astype(F32).astype(BF16)
        wide = dot(both, table)
        wide = wide[:capacity] + wide[capacity:]
        mine = iota(wide.shape, 0) == lax.rem(iota(wide.shape, 1), capacity)
        row = jnp.sum(jnp.where(mine, wide, 0.0), axis=0, keepdims=True).astype(jnp.int32)
        hot = (row == iota((groups, CHUNK), 0)).astype(F32).astype(BF16)
        out[:, pl.ds(first, CHUNK)] = hot


def column_table(wide, which, capacity, groups):
    index = column(wide, which, capacity).astype(jnp.int32)
    return (index == iota((wide.shape[0], groups), 1)).astype(F32).astype(BF16)


def set_gram(gram, pair, single):
    rank = gram.shape[0]
    ridge = jnp.where(iota((rank, rank), 0) == iota((rank, rank), 1), RIDGE, 0.0)
    high, middle, low = split3(gram + ridge)
    pair[...] = jnp.concatenate(
        [jnp.concatenate([high, middle], axis=1), jnp.concatenate([middle, high], axis=1)], axis=0
    )
    single[...] = jnp.concatenate([low, high], axis=0)


def gram_product(vector, pair, single):
    high, middle, low = split3(vector)
    first = dot(jnp.concatenate([high, middle], axis=1), pair[...])
    return halves(first) + dot(jnp.concatenate([high, low], axis=1), single[...])


def slot_pass(vector, rows_ref, scaled, coefs, hot, hot_t):
    slots, rank = scaled.shape
    capacity = rows_ref.shape[1]
    pieces = jnp.concatenate(split2(vector), axis=1)
    total = None
    for first in range(0, slots, CHUNK):
        part = pl.ds(first, CHUNK)
        rows = rows_ref[pl.ds(first // capacity, CHUNK // capacity)].reshape(CHUNK, rank)
        along = jnp.sum(rows * halves(dot(hot[part, :], pieces)), axis=1, keepdims=True)
        if coefs is None:
            terms = along * scaled[part, :]
        else:
            weighted = scaled[part, :] * rows
            scaled[part, :] = weighted
            terms = coefs[part, :] * rows - along * weighted
        folded = dot(hot_t[:, part], jnp.concatenate(split2(terms), axis=1))
        total = folded if total is None else total + folded
    return halves(total)


def conjugate_steps(x_ref, resid, direction, operate):
    def step(iteration, squares):
        p = direction[...]
        image = operate(p)
        alpha = squares / jnp.sum(p * image, axis=1, keepdims=True)
        x_ref[...] = x_ref[...] + alpha * p
        r = resid[...] - alpha * image
        resid[...] = r
        fresh = jnp.sum(r * r, axis=1, keepdims=True)
        direction[...] = r + (fresh / squares) * p
        return fresh

    r = resid[...]
    direction[...] = r
    lax.fori_loop(0, ITERS, step, jnp.sum(r * r, axis=1, keepdims=True))


def body(
    n,
    fast,
    capacity,
    user_hbm,
    item_hbm,
    rhs_hbm,
    user_gram,
    req_count,
    req_item,
    req_user,
    weight,
    rating,
    user_out,
    item_out,
    user_v,
    item_v,
    rhs_v,
    note_src,
    notes,
    part_src,
    parts,
    row_src,
    gram_rows,
    part2_src,
    parts2,
    row2_src,
    gram2_rows,
    found,
    fetched,
    outgoing,
    arrived,
    user_scaled,
    user_coefs,
    item_scaled,
    item_coefs,
    user_hot,
    user_hot_t,
    item_hot,
    item_hot_t,
    pair,
    single,
    user_r,
    user_p,
    item_r,
    item_p,
    send_sem,
    recv_sem,
    own_sem,
    load_sem,
):
    me = lax.axis_index("users") * fast + lax.axis_index("items")
    slots = n * capacity
    rank = user_out.shape[1]
    users, items = user_out.shape[0], item_out.shape[0]
    barrier = pltpu.get_barrier_semaphore()

    loads = [
        pltpu.make_async_copy(source, target, load_sem.at[index])
        for index, (source, target) in enumerate(
            ((item_hbm, item_v), (user_hbm, user_v), (rhs_hbm, rhs_v))
        )
    ]
    for load in loads:
        load.start()

    def place(step):
        peer = lax.rem(me + step, n)
        return peer, (lax.div(peer, fast), lax.rem(peer, fast))

    @pl.loop(1, n)
    def _(step):
        _, device = place(step)
        pl.semaphore_signal(barrier, inc=1, device_id=device, device_id_type=MESH)

    def block(source, index):
        return source.at[index] if source.shape[0] == n else source.at[0]

    def send(which, source, target):
        @pl.loop(1, n)
        def _(step):
            peer, device = place(step)
            pltpu.make_async_remote_copy(
                src_ref=block(source, peer),
                dst_ref=target.at[me],
                send_sem=send_sem.at[which],
                recv_sem=recv_sem.at[which],
                device_id=device,
                device_id_type=MESH,
            ).start()

        pltpu.make_async_copy(block(source, me), target.at[me], own_sem.at[which]).start()

    def arrive(which, source, target):
        span = target.at[pl.ds(0, n - 1)]
        pltpu.make_async_copy(span, span, recv_sem.at[which]).wait()
        pltpu.make_async_copy(block(source, me), target.at[me], own_sem.at[which]).wait()

    def sent(which, target):
        span = target.at[pl.ds(0, n - 1)]
        pltpu.make_async_copy(span, span, send_sem.at[which]).wait()

    live = iota((capacity, n), 0) < req_count[...]
    weights = jnp.where(live, weight[...], 0.0)
    coefs = jnp.where(live, (1.0 + weight[...]) * rating[...], 0.0)
    asked = req_item[...].astype(F32)
    members = req_user[...].astype(F32)
    rest = jnp.zeros((rank - 4 * capacity, n), F32)
    own_note = jnp.concatenate([asked, weights, coefs, members, rest], axis=0).T
    note_src[...] = own_note[:, None, :]
    pl.semaphore_wait(barrier, n - 1)
    send(0, note_src, notes)

    loads[0].wait()
    mine = item_v[...]
    partial = jnp.dot(mine.T, mine, precision=lax.Precision.HIGHEST, preferred_element_type=F32)
    part_src[...] = partial[:, None, :]
    send(1, part_src, parts)

    pieces = split3(own_note)
    for first in range(0, slots, CHUNK):
        part = pl.ds(first, CHUNK)
        wide = spread(pieces, first, CHUNK, capacity, n)
        user_scaled[part, :] = jnp.broadcast_to(column(wide, 1, capacity), (CHUNK, rank))
        user_coefs[part, :] = jnp.broadcast_to(column(wide, 2, capacity), (CHUNK, rank))
        user_hot[part, :] = column_table(wide, 3, capacity, users)
    row_table(members, users, capacity, user_hot_t)

    arrive(0, note_src, notes)
    all_notes = notes[:, 0, :]
    pieces = split3(all_notes)
    item_pieces = split3(item_v[...])
    item_pair = jnp.concatenate(item_pieces[:2], axis=1)
    for first in range(0, slots, CHUNK):
        part = pl.ds(first, CHUNK)
        wide = spread(pieces[:2], first, CHUNK, capacity, n)
        hot = column_table(wide, 0, capacity, items)
        item_hot[part, :] = hot
        picked = halves(dot(hot, item_pair)) + dot(hot, item_pieces[2])
        found[pl.ds(first // capacity, CHUNK // capacity)] = picked.reshape(
            CHUNK // capacity, capacity, rank
        )
    send(2, found, fetched)
    arrive(1, part_src, parts)
    row_src[...] = jnp.sum(parts[...], axis=0, keepdims=True)
    send(3, row_src, gram_rows)

    for first in range(0, slots, CHUNK):
        part = pl.ds(first, CHUNK)
        wide = spread(pieces, first, CHUNK, capacity, n)
        item_scaled[part, :] = jnp.broadcast_to(column(wide, 1, capacity), (CHUNK, rank))
        item_coefs[part, :] = jnp.broadcast_to(column(wide, 2, capacity), (CHUNK, rank))
    row_table(all_notes.T[:capacity], items, capacity, item_hot_t)

    loads[1].wait()
    arrive(2, found, fetched)
    start = user_v[...]
    right = slot_pass(start, fetched, user_scaled, user_coefs, user_hot, user_hot_t)
    arrive(3, row_src, gram_rows)
    set_gram(gram_rows[:, 0, :], pair, single)
    user_r[...] = right - gram_product(start, pair, single)
    user_v[...] = start

    def user_operate(vector):
        return gram_product(vector, pair, single) + slot_pass(
            vector, fetched, user_scaled, None, user_hot, user_hot_t
        )

    conjugate_steps(user_v, user_r, user_p, user_operate)
    refreshed = user_v[...]
    user_out[...] = refreshed

    partial = jnp.dot(
        refreshed.T, refreshed, precision=lax.Precision.HIGHEST, preferred_element_type=F32
    )
    part2_src[...] = partial[:, None, :]
    send(4, part2_src, parts2)
    user_pieces = split3(refreshed)
    user_pair = jnp.concatenate(user_pieces[:2], axis=1)
    for first in range(0, slots, CHUNK):
        hot = user_hot[pl.ds(first, CHUNK), :]
        picked = halves(dot(hot, user_pair)) + dot(hot, user_pieces[2])
        outgoing[pl.ds(first // capacity, CHUNK // capacity)] = picked.reshape(
            CHUNK // capacity, capacity, rank
        )
    send(5, outgoing, arrived)
    arrive(4, part2_src, parts2)
    row2_src[...] = jnp.sum(parts2[...], axis=0, keepdims=True)
    send(6, row2_src, gram2_rows)

    loads[2].wait()
    arrive(5, outgoing, arrived)
    start = item_v[...]
    right = rhs_v[...] + slot_pass(
        start, arrived, item_scaled, item_coefs, item_hot, item_hot_t
    )
    arrive(6, row2_src, gram2_rows)
    set_gram(user_gram[...] + gram2_rows[:, 0, :], pair, single)
    item_r[...] = right - gram_product(start, pair, single)
    item_out[...] = start

    def item_operate(vector):
        return gram_product(vector, pair, single) + slot_pass(
            vector, arrived, item_scaled, None, item_hot, item_hot_t
        )

    conjugate_steps(item_out, item_r, item_p, item_operate)
    for which, target in enumerate(
        (notes, parts, fetched, gram_rows, parts2, arrived, gram2_rows)
    ):
        sent(which, target)


def per_device(
    user_old, item_old, item_rhs, user_gram, req_count, req_item, req_user, weight, rating
):
    fast = lax.axis_size("items")
    n = lax.axis_size("users") * fast
    capacity = req_item.shape[2]
    users, rank = user_old.shape
    items = item_old.shape[0]
    slots = n * capacity
    vmem = pl.BlockSpec(memory_space=pltpu.VMEM)
    anywhere = pl.BlockSpec(memory_space=pl.ANY)
    row = pltpu.VMEM((1, 1, rank), F32)
    rows = pltpu.VMEM((n, 1, rank), F32)
    factors = pltpu.VMEM((n, capacity, rank), F32)
    scaled = pltpu.VMEM((slots, rank), F32)
    flip = lambda array: jnp.swapaxes(array[0], 0, 1)
    return pl.pallas_call(
        functools.partial(body, n, fast, capacity),
        out_shape=(
            jax.ShapeDtypeStruct((users, rank), F32),
            jax.ShapeDtypeStruct((items, rank), F32),
        ),
        in_specs=[anywhere] * 3 + [vmem] * 6,
        out_specs=(vmem, vmem),
        scratch_shapes=[
            pltpu.VMEM((users, rank), F32),
            pltpu.VMEM((items, rank), F32),
            pltpu.VMEM((items, rank), F32),
            rows,
            rows,
            rows,
            rows,
            row,
            rows,
            rows,
            rows,
            row,
            rows,
            factors,
            factors,
            factors,
            factors,
            scaled,
            scaled,
            scaled,
            scaled,
            pltpu.VMEM((slots, users), BF16),
            pltpu.VMEM((users, slots), BF16),
            pltpu.VMEM((slots, items), BF16),
            pltpu.VMEM((items, slots), BF16),
            pltpu.VMEM((2 * rank, 2 * rank), BF16),
            pltpu.VMEM((2 * rank, rank), BF16),
            pltpu.VMEM((users, rank), F32),
            pltpu.VMEM((users, rank), F32),
            pltpu.VMEM((items, rank), F32),
            pltpu.VMEM((items, rank), F32),
            pltpu.SemaphoreType.DMA((7,)),
            pltpu.SemaphoreType.DMA((7,)),
            pltpu.SemaphoreType.DMA((7,)),
            pltpu.SemaphoreType.DMA((3,)),
        ],
        compiler_params=pltpu.CompilerParams(
            collective_id=0, has_side_effects=True, vmem_limit_bytes=40 * 2**20
        ),
    )(
        user_old,
        item_old,
        item_rhs,
        user_gram,
        req_count,
        flip(req_item),
        flip(req_user),
        flip(weight),
        flip(rating),
    )


def solution(mesh):
    in_specs = (
        P(("users", "items"), None),
        P(("users", "items"), None),
        P(("users", "items"), None),
        P(),
        P(("users", "items"), None),
        P(("users", "items"), None, None),
        P(("users", "items"), None, None),
        P(("users", "items"), None, None),
        P(("users", "items"), None, None),
    )
    out_specs = (P(("users", "items"), None), P(("users", "items"), None))
    return jax.shard_map(
        per_device, mesh=mesh, in_specs=in_specs, out_specs=out_specs, check_vma=False
    )
```

time: 430 us -> 98 us (0.23)
  waiting for transfers between devices: 278 us -> 0 us
  Pallas kernels: 0 us -> 88.5 us
  matrix products: 84 us -> 0 us
  blocking collectives: 20.9 us -> 0 us
  between operations: 15.3 us -> 0.66 us
  starting transfers between devices: 13.6 us -> 0 us
  other arithmetic: 8.73 us -> 0 us
    psum x2 -> x0, waiting for transfers between devices: 261 us -> none  [the longest x1 144 us: per_device(): lax.psum(jnp.dot(user_new.T, user_new, precision=highest), ('users', 'ite...]
    pallas_call x0 -> x1, Pallas kernels: none -> 88.5 us  [per_device(): pl.pallas_call(functools.partial(body, n, fast, capacity), out_shape=(jax...]
    dot_general x59 -> x0, matrix products: 84 us -> none  [the longest x19 39.7 us: pick_rows(): return jnp.dot(table, source, precision=highest)]
    all_to_all x1 -> x0, blocking collectives: 20.9 us -> none  [per_device(): lax.all_to_all(req_item[0], ('users', 'items'), split_axis=0, concat_axis...]
    all_to_all x3 -> x0, waiting for transfers between devices: 16.6 us -> none  [the longest x1 16.6 us: per_device(): lax.all_to_all(found, ('users', 'items'), split_axis=0, concat_axis=0, ti...]
    all_to_all x3 -> x0, starting transfers between devices: 13.5 us -> none  [the longest x1 5.1 us: per_device(): lax.all_to_all(outgoing, ('users', 'items'), split_axis=0, concat_axis=0,...]
    unnamed x27 -> x20, local copies, waits for them, and re-layouts: 3.08 us -> 8.44 us
  transfers between devices with their start and end apart: 5 -> 0, of which waited for: 3 -> 0; matrix products, arithmetic and copies ran while one was open for 10% -> 0% of each run, Pallas kernels for 0% -> 0%
where the time goes in v1:
time: 98 us; the launch traced here: 97.6 us
  Pallas kernels  88.5 us (90%)
  local copies, waits for them, and re-layouts  8.44 us (9%)
    pallas_call x1, Pallas kernels, per_device(): pl.pallas_call(functools.partial(body, n, fast, capacity), out_shape=(jax...  88.5 us
    unnamed x20, local copies, waits for them, and re-layouts  8.44 us

profile of v1, /device:TPU:1, one launch (start us, length us, event | category | flops | bytes accessed | tf_op | source)
XLA Modules:
  0.0 97.6 jit_solution(5425690445726055168)
XLA Ops:
  0.6 0.0 copy-start.8
  0.6 0.6 copy-done.8
  1.3 0.0 copy-start
  1.3 0.9 copy-done
  2.2 0.0 copy-start.1
  2.2 0.9 copy-done.1
  3.2 0.0 copy-start.2
  3.2 0.9 copy-done.2
  4.1 0.0 copy-start.3
  4.1 0.8 copy-done.3
  4.9 0.0 copy-start.4
  4.9 0.7 copy-done.4
  5.6 0.0 copy-start.5
  5.6 0.7 copy-done.5
  6.3 0.0 copy-start.6
  6.3 0.7 copy-done.6
  7.0 0.0 copy-start.7
  7.0 0.7 copy-done.7
  7.7 88.5 %shard_map.104 = (f32[256,128]{1,0:T(8,128)S(1)}, f32[512,128]{1,0:T(8,128)S(1)}) custom-call(f32[256,128]{1,0:T(8,128)S(1)} %copy-done.2, f32[512,128]{1,0:T(8,128)S(1)} %copy-done, f32[512,128]{1,0:T(8,128)S(1)} %copy-done.1, f32[128,128]{1,0:T(8,128)S(1)} %copy-done.3, s32[1,128]{1,0:T(1,128)S(1)} %copy-done.8, s32[16,128]{1,0:T(8,128)S(1)} %bitcast.12, ...), custom_call_target="tpu_custom_call" | custom-call | tf_op jit(solution)/shard_map/pallas_call | solution.py:362
  96.2 0.7 copy.13
  96.9 0.7 copy.14
Async XLA Ops:
  0.6 0.7 copy-start.8
  1.3 0.9 copy-start
  2.2 0.9 copy-start.1
  3.2 0.9 copy-start.2
  4.1 0.8 copy-start.3
  4.9 0.7 copy-start.4
  5.6 0.7 copy-start.5
  6.3 0.7 copy-start.6
  7.0 0.7 copy-start.7

commit v2 on v1

v2 whole, which is shorter than its diff:
```python
import functools
from typing import Any, NamedTuple
import jax
import jax.numpy as jnp
from jax import lax
from jax.sharding import PartitionSpec as P
from jax.experimental import pallas as pl
from jax.experimental.pallas import tpu as pltpu

ITERS = 8
RIDGE = 1.0
CHUNK = 512
PICK = 128
MESH = pl.DeviceIdType.MESH
F32 = jnp.float32
BF16 = jnp.bfloat16


def split2(value):
    high = value.astype(BF16)
    return high, (value - high.astype(F32)).astype(BF16)


def split3(value):
    high = value.astype(BF16)
    rest = value - high.astype(F32)
    middle = rest.astype(BF16)
    return high, middle, (rest - middle.astype(F32)).astype(BF16)


def dot(left, right):
    return jnp.dot(left, right, preferred_element_type=F32)


def halves(value):
    width = value.shape[1] // 2
    return value[:, :width] + value[:, width:]


def iota(shape, axis):
    return lax.broadcasted_iota(jnp.int32, shape, axis)


def owner_table(first, rows, capacity, senders):
    owner = lax.div(iota((rows, senders), 0), capacity) + first
    return (owner == iota((rows, senders), 1)).astype(F32).astype(BF16)


def spread(pieces, first, rows, capacity, senders):
    table = owner_table(first, rows, capacity, senders)
    wide = halves(dot(table, jnp.concatenate(pieces[:2], axis=1)))
    if len(pieces) > 2:
        wide = wide + dot(table, pieces[2])
    return wide


def column(wide, which, capacity):
    slot = lax.rem(iota(wide.shape, 0), capacity) + which * capacity
    return jnp.sum(jnp.where(slot == iota(wide.shape, 1), wide, 0.0), axis=1, keepdims=True)


def row_table(indices, groups, capacity, out):
    senders = indices.shape[1]
    both = jnp.concatenate(split2(indices), axis=0)
    slots = senders * capacity
    for first in range(0, slots, CHUNK):
        owner = lax.div(iota((senders, CHUNK), 1), capacity) + first // capacity
        table = (owner == iota((senders, CHUNK), 0)).astype(F32).astype(BF16)
        wide = dot(both, table)
        wide = wide[:capacity] + wide[capacity:]
        mine = iota(wide.shape, 0) == lax.rem(iota(wide.shape, 1), capacity)
        row = jnp.sum(jnp.where(mine, wide, 0.0), axis=0, keepdims=True).astype(jnp.int32)
        hot = (row == iota((groups, CHUNK), 0)).astype(F32).astype(BF16)
        out[:, pl.ds(first, CHUNK)] = hot


def column_table(wide, which, capacity, groups):
    index = column(wide, which, capacity).astype(jnp.int32)
    return (index == iota((wide.shape[0], groups), 1)).astype(F32).astype(BF16)


def set_gram(gram, pair, single):
    rank = gram.shape[0]
    ridge = jnp.where(iota((rank, rank), 0) == iota((rank, rank), 1), RIDGE, 0.0)
    high, middle, low = split3(gram + ridge)
    pair[...] = jnp.concatenate(
        [jnp.concatenate([high, middle], axis=1), jnp.concatenate([middle, high], axis=1)], axis=0
    )
    single[...] = jnp.concatenate([low, high], axis=0)


class State(NamedTuple):
    x: Any
    r: Any
    p: Any
    squares: Any
    pieces: Any
    terms: Any
    pair: Any
    single: Any
    block: int


def pick_terms(state, rows_ref, scaled, coefs, hot):
    slots, rank = scaled.shape
    capacity = rows_ref.shape[1]
    for first in range(0, slots, PICK):
        part = pl.ds(first, PICK)
        rows = rows_ref[pl.ds(first // capacity, PICK // capacity)].reshape(PICK, rank)
        picked = halves(dot(hot[part, :], state.pieces[:, : 2 * rank]))
        along = jnp.sum(rows * picked, axis=1, keepdims=True)
        if coefs is None:
            terms = along * scaled[part, :]
        else:
            weighted = scaled[part, :] * rows
            scaled[part, :] = weighted
            terms = coefs[part, :] * rows - along * weighted
        high, low = split2(terms)
        state.terms[part, :rank] = high
        state.terms[part, rank:] = low


def keep_pieces(state, part, value):
    rank = value.shape[1]
    for index, piece in enumerate(split3(value)):
        state.pieces[part, index * rank : (index + 1) * rank] = piece


def gram_part(state, part, rank):
    mine = state.pieces[part, :]
    first = dot(mine[:, : 2 * rank], state.pair[...])
    outer = jnp.concatenate([mine[:, :rank], mine[:, 2 * rank :]], axis=1)
    return halves(first) + dot(outer, state.single[...])


def begin(state, rows_ref, scaled, coefs, hot):
    keep_pieces(state, slice(None), state.x[...])
    pick_terms(state, rows_ref, scaled, coefs, hot)


def conjugate_steps(state, base, rows_ref, scaled, hot, hot_t):
    groups, rank = state.x.shape
    for first in range(0, groups, state.block):
        part = pl.ds(first, state.block)
        r = halves(dot(hot_t[part, :], state.terms[...])) - gram_part(state, part, rank)
        if base is not None:
            r = r + base[part, :]
        state.r[part, :] = r
        state.p[part, :] = r
        squares = jnp.sum(r * r, axis=1, keepdims=True)
        state.squares[part, :] = jnp.broadcast_to(squares, r.shape)
    keep_pieces(state, slice(None), state.p[...])

    def step(iteration, carry):
        pick_terms(state, rows_ref, scaled, None, hot)
        for first in range(0, groups, state.block):
            part = pl.ds(first, state.block)
            image = halves(dot(hot_t[part, :], state.terms[...])) + gram_part(state, part, rank)
            p = state.p[part, :]
            squares = state.squares[part, :]
            alpha = squares / jnp.sum(p * image, axis=1, keepdims=True)
            state.x[part, :] = state.x[part, :] + alpha * p
            r = state.r[part, :] - alpha * image
            state.r[part, :] = r
            fresh = jnp.sum(r * r, axis=1, keepdims=True)
            p = r + (fresh / squares) * p
            state.p[part, :] = p
            state.squares[part, :] = jnp.broadcast_to(fresh, p.shape)
            keep_pieces(state, part, p)
        return carry

    lax.fori_loop(0, ITERS, step, 0)


def body(
    n,
    fast,
    capacity,
    user_in,
    item_in,
    rhs_in,
    user_gram_in,
    count_in,
    asked_in,
    members_in,
    weight_in,
    rating_in,
    user_out,
    item_out,
    item_v,
    rhs_v,
    user_gram,
    count_v,
    asked_v,
    members_v,
    weight_v,
    rating_v,
    note_src,
    notes,
    partial,
    near,
    across,
    whole,
    partial2,
    near2,
    across2,
    whole2,
    found,
    fetched,
    outgoing,
    arrived,
    user_scaled,
    user_coefs,
    item_scaled,
    item_coefs,
    user_hot,
    user_hot_t,
    item_hot,
    item_hot_t,
    pair,
    single,
    terms,
    user_r,
    user_p,
    user_squares,
    user_pieces,
    item_r,
    item_p,
    item_squares,
    item_pieces,
    send_sem,
    recv_sem,
    own_sem,
    load_sem,
):
    me = lax.axis_index("users") * fast + lax.axis_index("items")
    slots = n * capacity
    users, rank = user_out.shape
    items = item_out.shape[0]
    inner = near.shape[0]
    outer = across.shape[0]
    band = rank // inner
    seat, team = lax.rem(me, inner), lax.div(me, inner)
    region = CHUNK // capacity
    barrier = pltpu.get_barrier_semaphore()

    loads = [
        pltpu.make_async_copy(source, target, load_sem.at[index])
        for index, (source, target) in enumerate(
            (
                (count_in, count_v),
                (asked_in, asked_v),
                (members_in, members_v),
                (weight_in, weight_v),
                (rating_in, rating_v),
                (item_in, item_v),
                (user_in, user_out),
                (rhs_in, rhs_v),
                (user_gram_in, user_gram),
                (item_in, item_out),
            )
        )
    ]
    for load in loads:
        load.start()

    def at(peer):
        return (lax.div(peer, fast), lax.rem(peer, fast))

    @pl.loop(1, n)
    def _(step):
        pl.semaphore_signal(
            barrier, inc=1, device_id=at(lax.rem(me + step, n)), device_id_type=MESH
        )

    def push(which, source, target, peer):
        pltpu.make_async_remote_copy(
            src_ref=source,
            dst_ref=target,
            send_sem=send_sem.at[which],
            recv_sem=recv_sem.at[which],
            device_id=at(peer),
            device_id_type=MESH,
        ).start()

    def landed(which, target):
        span = target.at[pl.ds(0, target.shape[0] - 1)]
        pltpu.make_async_copy(span, span, recv_sem.at[which]).wait()

    def sent(which, target):
        span = target.at[pl.ds(0, target.shape[0] - 1)]
        pltpu.make_async_copy(span, span, send_sem.at[which]).wait()

    def own(which, source, target):
        return pltpu.make_async_copy(source.at[me], target.at[me], own_sem.at[which])

    def gram_near(which, source, first):
        first[seat] = source[pl.ds(pl.multiple_of(seat * band, band), band), :]

        @pl.loop(1, inner)
        def _(step):
            other = lax.rem(seat + step, inner)
            push(
                which,
                source.at[pl.ds(pl.multiple_of(other * band, band), band)],
                first.at[seat],
                team * inner + other,
            )

    def gram_across(which, first, second):
        landed(which, first)
        second[team] = jnp.sum(first[...], axis=0)

        @pl.loop(1, outer)
        def _(step):
            other = lax.rem(team + step, outer)
            push(which + 1, second.at[team], second.at[team], other * inner + seat)

    def gram_back(which, second, third):
        landed(which + 1, second)
        third[seat] = jnp.sum(second[...], axis=0)

        @pl.loop(1, inner)
        def _(step):
            other = lax.rem(seat + step, inner)
            push(which + 2, third.at[seat], third.at[seat], team * inner + other)

    def gram_value(which, third):
        landed(which + 2, third)
        return third[...].reshape(rank, rank)

    def send_region(which, source, target, base):
        @pl.loop(0, region)
        def _(step):
            peer = base + lax.rem(me + step, region)

            @pl.when(peer != me)
            def _():
                push(which, source.at[peer], target.at[me], peer)

    def turn(step):
        return lax.rem(lax.axis_index("items") + step, slots // CHUNK)

    for load in loads[:5]:
        load.wait()
    live = iota((capacity, n), 0) < count_v[...]
    weights = jnp.where(live, weight_v[...], 0.0)
    coefs = jnp.where(live, (1.0 + weight_v[...]) * rating_v[...], 0.0)
    asked = asked_v[...].astype(F32)
    members = members_v[...].astype(F32)
    rest = jnp.zeros((rank - 4 * capacity, n), F32)
    own_note = jnp.concatenate([asked, weights, coefs, members, rest], axis=0).T
    note_src[...] = own_note[:, None, :]
    loads[5].wait()
    mine = item_v[...]
    partial[...] = jnp.dot(
        mine.T, mine, precision=lax.Precision.HIGHEST, preferred_element_type=F32
    )
    pl.semaphore_wait(barrier, n - 1)

    @pl.loop(1, n)
    def _(step):
        peer = lax.rem(me + step, n)
        push(0, note_src.at[peer], notes.at[me], peer)

    own(0, note_src, notes).start()
    gram_near(3, partial, near)

    pieces = split3(own_note)
    for first in range(0, slots, CHUNK):
        part = pl.ds(first, CHUNK)
        wide = spread(pieces, first // capacity, CHUNK, capacity, n)
        user_scaled[part, :] = jnp.broadcast_to(column(wide, 1, capacity), (CHUNK, rank))
        user_coefs[part, :] = jnp.broadcast_to(column(wide, 2, capacity), (CHUNK, rank))
        user_hot[part, :] = column_table(wide, 3, capacity, users)
    gram_across(3, near, across)
    row_table(members, users, capacity, user_hot_t)

    own(0, note_src, notes).wait()
    landed(0, notes)
    all_notes = notes[:, 0, :]
    pieces = split3(all_notes)
    item_split = split3(item_v[...])
    item_pair = jnp.concatenate(item_split[:2], axis=1)
    for step in range(slots // CHUNK):
        base = pl.multiple_of(turn(step) * region, region)
        wide = spread(pieces[:2], base, CHUNK, capacity, n)
        hot = column_table(wide, 0, capacity, items)
        item_hot[pl.ds(pl.multiple_of(base * capacity, CHUNK), CHUNK), :] = hot
        picked = halves(dot(hot, item_pair)) + dot(hot, item_split[2])
        found[pl.ds(base, region)] = picked.reshape(region, capacity, rank)
        send_region(1, found, fetched, base)
        if step == 0:
            gram_back(3, across, whole)
    own(1, found, fetched).start()

    for first in range(0, slots, CHUNK):
        part = pl.ds(first, CHUNK)
        wide = spread(pieces, first // capacity, CHUNK, capacity, n)
        item_scaled[part, :] = jnp.broadcast_to(column(wide, 1, capacity), (CHUNK, rank))
        item_coefs[part, :] = jnp.broadcast_to(column(wide, 2, capacity), (CHUNK, rank))
    row_table(all_notes.T[:capacity], items, capacity, item_hot_t)

    loads[6].wait()
    state = State(
        user_out, user_r, user_p, user_squares, user_pieces, terms, pair, single, users // 2
    )
    own(1, found, fetched).wait()
    landed(1, fetched)
    begin(state, fetched, user_scaled, user_coefs, user_hot)
    set_gram(gram_value(3, whole), pair, single)
    conjugate_steps(state, None, fetched, user_scaled, user_hot, user_hot_t)

    refreshed = user_out[...]
    partial2[...] = jnp.dot(
        refreshed.T, refreshed, precision=lax.Precision.HIGHEST, preferred_element_type=F32
    )
    gram_near(6, partial2, near2)
    user_split = split3(refreshed)
    user_pair = jnp.concatenate(user_split[:2], axis=1)
    for step in range(slots // CHUNK):
        base = pl.multiple_of(turn(step) * region, region)
        hot = user_hot[pl.ds(pl.multiple_of(base * capacity, CHUNK), CHUNK), :]
        picked = halves(dot(hot, user_pair)) + dot(hot, user_split[2])
        outgoing[pl.ds(base, region)] = picked.reshape(region, capacity, rank)
        send_region(2, outgoing, arrived, base)
        if step == 1:
            gram_across(6, near2, across2)
        if step == 2:
            gram_back(6, across2, whole2)
    own(2, outgoing, arrived).start()

    for load in loads[7:]:
        load.wait()
    state = State(
        item_out, item_r, item_p, item_squares, item_pieces, terms, pair, single, items // 2
    )
    set_gram(user_gram[...] + gram_value(6, whole2), pair, single)
    own(2, outgoing, arrived).wait()
    landed(2, arrived)
    begin(state, arrived, item_scaled, item_coefs, item_hot)
    conjugate_steps(state, rhs_v, arrived, item_scaled, item_hot, item_hot_t)
    for which, target in enumerate(
        (notes, fetched, arrived, near, across, whole, near2, across2, whole2)
    ):
        sent(which, target)


def per_device(
    user_old, item_old, item_rhs, user_gram, req_count, req_item, req_user, weight, rating
):
    fast = lax.axis_size("items")
    n = lax.axis_size("users") * fast
    capacity = req_item.shape[2]
    users, rank = user_old.shape
    items = item_old.shape[0]
    slots = n * capacity
    inner = 2 * fast
    outer = n // inner
    vmem = pl.BlockSpec(memory_space=pltpu.VMEM)
    hbm = pl.BlockSpec(memory_space=pltpu.HBM)

    def floats(*shape):
        return pltpu.VMEM(shape, F32)

    gram = [
        floats(rank, rank),
        floats(inner, rank // inner, rank),
        floats(outer, rank // inner, rank),
        floats(inner, rank // inner, rank),
    ]
    flip = lambda array: jnp.swapaxes(array[0], 0, 1)
    return pl.pallas_call(
        functools.partial(body, n, fast, capacity),
        out_shape=(
            jax.ShapeDtypeStruct((users, rank), F32),
            jax.ShapeDtypeStruct((items, rank), F32),
        ),
        in_specs=[hbm] * 9,
        out_specs=(vmem, vmem),
        scratch_shapes=[
            floats(items, rank),
            floats(items, rank),
            floats(rank, rank),
            pltpu.VMEM((1, n), jnp.int32),
            pltpu.VMEM((capacity, n), jnp.int32),
            pltpu.VMEM((capacity, n), jnp.int32),
            floats(capacity, n),
            floats(capacity, n),
            floats(n, 1, rank),
            floats(n, 1, rank),
            *gram,
            *gram,
            *[floats(n, capacity, rank)] * 4,
            *[floats(slots, rank)] * 4,
            pltpu.VMEM((slots, users), BF16),
            pltpu.VMEM((users, slots), BF16),
            pltpu.VMEM((slots, items), BF16),
            pltpu.VMEM((items, slots), BF16),
            pltpu.VMEM((2 * rank, 2 * rank), BF16),
            pltpu.VMEM((2 * rank, rank), BF16),
            pltpu.VMEM((slots, 2 * rank), BF16),
            *[floats(users, rank)] * 3,
            pltpu.VMEM((users, 3 * rank), BF16),
            *[floats(items, rank)] * 3,
            pltpu.VMEM((items, 3 * rank), BF16),
            pltpu.SemaphoreType.DMA((9,)),
            pltpu.SemaphoreType.DMA((9,)),
            pltpu.SemaphoreType.DMA((3,)),
            pltpu.SemaphoreType.DMA((10,)),
        ],
        compiler_params=pltpu.CompilerParams(
            collective_id=0, has_side_effects=True, vmem_limit_bytes=60 * 2**20
        ),
    )(
        user_old,
        item_old,
        item_rhs,
        user_gram,
        req_count,
        flip(req_item),
        flip(req_user),
        flip(weight),
        flip(rating),
    )


def solution(mesh):
    in_specs = (
        P(("users", "items"), None),
        P(("users", "items"), None),
        P(("users", "items"), None),
        P(),
        P(("users", "items"), None),
        P(("users", "items"), None, None),
        P(("users", "items"), None, None),
        P(("users", "items"), None, None),
        P(("users", "items"), None, None),
    )
    out_specs = (P(("users", "items"), None), P(("users", "items"), None))
    return jax.shard_map(
        per_device, mesh=mesh, in_specs=in_specs, out_specs=out_specs, check_vma=False
    )
```

time: 98 us -> 82.1 us (0.84)
  Pallas kernels: 88.5 us -> 79 us
  local copies, waits for them, and re-layouts: 8.44 us -> 2.32 us
    pallas_call x1, Pallas kernels: 88.5 us -> 79 us  [per_device(): pl.pallas_call(functools.partial(body, n, fast, capacity), out_shape=(jax...]
    unnamed x20 -> x4, local copies, waits for them, and re-layouts: 8.44 us -> 2.32 us
where the time goes in v2:
time: 82.1 us; the launch traced here: 82 us
  Pallas kernels  79 us (96%)
  local copies, waits for them, and re-layouts  2.32 us (3%)
    pallas_call x1, Pallas kernels, per_device(): pl.pallas_call(functools.partial(body, n, fast, capacity), out_shape=(jax...  79 us
    unnamed x4, local copies, waits for them, and re-layouts  2.32 us

profile of v2, /device:TPU:1, one launch (start us, length us, event | category | flops | bytes accessed | tf_op | source)
XLA Modules:
  0.0 82.0 jit_solution(3639442885148629661)
XLA Ops:
  0.6 79.0 %shard_map.104 = (f32[256,128]{1,0:T(8,128)}, f32[512,128]{1,0:T(8,128)}) custom-call(f32[256,128]{1,0:T(8,128)} %user_in.1, f32[512,128]{1,0:T(8,128)} %item_in.1, f32[512,128]{1,0:T(8,128)} %rhs_in.1, f32[128,128]{1,0:T(8,128)} %user_gram_in.1, s32[1,128]{1,0:T(1,128)} %count_in.1, s32[16,128]{1,0:T(8,128)} %bitcast.12, s32[16,128]{1,0:T(8,128)} %bitcast.13, ...), custom_call_target="tpu_custom_call" | custom-call | tf_op jit(solution)/shard_map/pallas_call | solution.py:473
  79.7 0.0 copy-start
  79.7 1.6 %copy.13 = f32[256,128]{1,0:T(8,128)} copy(f32[256,128]{1,0:T(8,128)} %get-tuple-element.4) | data formatting | bytes 262144
  81.3 0.0 copy-done
  81.3 0.7 copy.14
Async XLA Ops:
  79.7 1.6 %copy-start = (f32[512,128]{1,0:T(8,128)S(1)}, f32[512,128]{1,0:T(8,128)}, u32[]{:S(2)}) copy-start(f32[512,128]{1,0:T(8,128)} %get-tuple-element.5) | copy-start | bytes 786436

commit v3 on v2

--- a/solution.py
+++ b/solution.py
@@ -133,11 +133,6 @@
     return halves(first) + dot(outer, state.single[...])
 
 
-def begin(state, rows_ref, scaled, coefs, hot):
-    keep_pieces(state, slice(None), state.x[...])
-    pick_terms(state, rows_ref, scaled, coefs, hot)
-
-
 def conjugate_steps(state, base, rows_ref, scaled, hot, hot_t):
     groups, rank = state.x.shape
     for first in range(0, groups, state.block):
@@ -151,7 +146,7 @@
         state.squares[part, :] = jnp.broadcast_to(squares, r.shape)
     keep_pieces(state, slice(None), state.p[...])
 
-    def step(iteration, carry):
+    def step(last):
         pick_terms(state, rows_ref, scaled, None, hot)
         for first in range(0, groups, state.block):
             part = pl.ds(first, state.block)
@@ -159,7 +154,11 @@
             p = state.p[part, :]
             squares = state.squares[part, :]
             alpha = squares / jnp.sum(p * image, axis=1, keepdims=True)
-            state.x[part, :] = state.x[part, :] + alpha * p
+            x = state.x[part, :] + alpha * p
+            state.x[part, :] = x
+            if last:
+                keep_pieces(state, part, x)
+                continue
             r = state.r[part, :] - alpha * image
             state.r[part, :] = r
             fresh = jnp.sum(r * r, axis=1, keepdims=True)
@@ -167,9 +166,13 @@
             state.p[part, :] = p
             state.squares[part, :] = jnp.broadcast_to(fresh, p.shape)
             keep_pieces(state, part, p)
+
+    def middle(iteration, carry):
+        step(False)
         return carry
 
-    lax.fori_loop(0, ITERS, step, 0)
+    lax.fori_loop(0, ITERS - 1, middle, 0)
+    step(True)
 
 
 def body(
@@ -196,6 +199,8 @@
     weight_v,
     rating_v,
     note_src,
+    gathered,
+    relay,
     notes,
     partial,
     near,
@@ -267,11 +272,17 @@
     def at(peer):
         return (lax.div(peer, fast), lax.rem(peer, fast))
 
-    @pl.loop(1, n)
-    def _(step):
-        pl.semaphore_signal(
-            barrier, inc=1, device_id=at(lax.rem(me + step, n)), device_id_type=MESH
-        )
+    def mate(step):
+        return team * inner + lax.rem(seat + step, inner)
+
+    def counterpart(step):
+        return lax.rem(team + step, outer) * inner + seat
+
+    for count, other in ((inner, mate), (outer, counterpart)):
+
+        @pl.loop(1, count)
+        def _(step):
+            pl.semaphore_signal(barrier, inc=1, device_id=at(other(step)), device_id_type=MESH)
 
     def push(which, source, target, peer):
         pltpu.make_async_remote_copy(
@@ -350,50 +361,67 @@
     members = members_v[...].astype(F32)
     rest = jnp.zeros((rank - 4 * capacity, n), F32)
     own_note = jnp.concatenate([asked, weights, coefs, members, rest], axis=0).T
-    note_src[...] = own_note[:, None, :]
+    for index in range(outer):
+        note_src[:, index, :] = own_note[index * inner : (index + 1) * inner]
+    pl.semaphore_wait(barrier, inner + outer - 2)
+
+    @pl.loop(1, inner)
+    def _(step):
+        other = lax.rem(seat + step, inner)
+        push(0, note_src.at[other], gathered.at[seat], mate(step))
+
+    gathered[seat] = note_src[seat]
     loads[5].wait()
     mine = item_v[...]
     partial[...] = jnp.dot(
         mine.T, mine, precision=lax.Precision.HIGHEST, preferred_element_type=F32
     )
-    pl.semaphore_wait(barrier, n - 1)
-
-    @pl.loop(1, n)
+    landed(0, gathered)
+    for index in range(outer):
+        relay[index] = gathered[:, index, :]
+
+    @pl.loop(1, outer)
     def _(step):
-        peer = lax.rem(me + step, n)
-        push(0, note_src.at[peer], notes.at[me], peer)
-
-    own(0, note_src, notes).start()
+        other = lax.rem(team + step, outer)
+        push(9, relay.at[other], notes.at[team], counterpart(step))
+
+    notes[team] = relay[team]
     gram_near(3, partial, near)
-
-    pieces = split3(own_note)
-    for first in range(0, slots, CHUNK):
-        part = pl.ds(first, CHUNK)
-        wide = spread(pieces, first // capacity, CHUNK, capacity, n)
-        user_scaled[part, :] = jnp.broadcast_to(column(wide, 1, capacity), (CHUNK, rank))
-        user_coefs[part, :] = jnp.broadcast_to(column(wide, 2, capacity), (CHUNK, rank))
-        user_hot[part, :] = column_table(wide, 3, capacity, users)
+    user_state = State(
+        user_out, user_r, user_p, user_squares, user_pieces, terms, pair, single, users // 2
+    )
+    item_state = State(
+        item_out, item_r, item_p, item_squares, item_pieces, terms, pair, single, items // 2
+    )
+    keep_pieces(item_state, slice(None), item_v[...])
+
+    landed(9, notes)
     gram_across(3, near, across)
-    row_table(members, users, capacity, user_hot_t)
-
-    own(0, note_src, notes).wait()
-    landed(0, notes)
-    all_notes = notes[:, 0, :]
+    all_notes = notes[...].reshape(n, rank)
     pieces = split3(all_notes)
-    item_split = split3(item_v[...])
-    item_pair = jnp.concatenate(item_split[:2], axis=1)
     for step in range(slots // CHUNK):
         base = pl.multiple_of(turn(step) * region, region)
         wide = spread(pieces[:2], base, CHUNK, capacity, n)
         hot = column_table(wide, 0, capacity, items)
         item_hot[pl.ds(pl.multiple_of(base * capacity, CHUNK), CHUNK), :] = hot
-        picked = halves(dot(hot, item_pair)) + dot(hot, item_split[2])
+        picked = halves(dot(hot, item_pieces[:, : 2 * rank]))
+        picked = picked + dot(hot, item_pieces[:, 2 * rank :])
         found[pl.ds(base, region)] = picked.reshape(region, capacity, rank)
+        if step == 1:
+            gram_back(3, across, whole)
         send_region(1, found, fetched, base)
-        if step == 0:
-            gram_back(3, across, whole)
     own(1, found, fetched).start()
 
+    own_pieces = split3(own_note)
+    for first in range(0, slots, CHUNK):
+        part = pl.ds(first, CHUNK)
+        wide = spread(own_pieces, first // capacity, CHUNK, capacity, n)
+        user_scaled[part, :] = jnp.broadcast_to(column(wide, 1, capacity), (CHUNK, rank))
+        user_coefs[part, :] = jnp.broadcast_to(column(wide, 2, capacity), (CHUNK, rank))
+        user_hot[part, :] = column_table(wide, 3, capacity, users)
+    row_table(members, users, capacity, user_hot_t)
+    loads[6].wait()
+    set_gram(gram_value(3, whole), pair, single)
     for first in range(0, slots, CHUNK):
         part = pl.ds(first, CHUNK)
         wide = spread(pieces, first // capacity, CHUNK, capacity, n)
@@ -401,47 +429,38 @@
         item_coefs[part, :] = jnp.broadcast_to(column(wide, 2, capacity), (CHUNK, rank))
     row_table(all_notes.T[:capacity], items, capacity, item_hot_t)
 
-    loads[6].wait()
-    state = State(
-        user_out, user_r, user_p, user_squares, user_pieces, terms, pair, single, users // 2
-    )
+    keep_pieces(user_state, slice(None), user_out[...])
     own(1, found, fetched).wait()
     landed(1, fetched)
-    begin(state, fetched, user_scaled, user_coefs, user_hot)
-    set_gram(gram_value(3, whole), pair, single)
-    conjugate_steps(state, None, fetched, user_scaled, user_hot, user_hot_t)
+    pick_terms(user_state, fetched, user_scaled, user_coefs, user_hot)
+    conjugate_steps(user_state, None, fetched, user_scaled, user_hot, user_hot_t)
 
     refreshed = user_out[...]
     partial2[...] = jnp.dot(
         refreshed.T, refreshed, precision=lax.Precision.HIGHEST, preferred_element_type=F32
     )
     gram_near(6, partial2, near2)
-    user_split = split3(refreshed)
-    user_pair = jnp.concatenate(user_split[:2], axis=1)
     for step in range(slots // CHUNK):
         base = pl.multiple_of(turn(step) * region, region)
         hot = user_hot[pl.ds(pl.multiple_of(base * capacity, CHUNK), CHUNK), :]
-        picked = halves(dot(hot, user_pair)) + dot(hot, user_split[2])
+        picked = halves(dot(hot, user_pieces[:, : 2 * rank]))
+        picked = picked + dot(hot, user_pieces[:, 2 * rank :])
         outgoing[pl.ds(base, region)] = picked.reshape(region, capacity, rank)
-        send_region(2, outgoing, arrived, base)
         if step == 1:
             gram_across(6, near2, across2)
-        if step == 2:
-            gram_back(6, across2, whole2)
+        send_region(2, outgoing, arrived, base)
     own(2, outgoing, arrived).start()
+    gram_back(6, across2, whole2)
 
     for load in loads[7:]:
         load.wait()
-    state = State(
-        item_out, item_r, item_p, item_squares, item_pieces, terms, pair, single, items // 2
-    )
-    set_gram(user_gram[...] + gram_value(6, whole2), pair, single)
     own(2, outgoing, arrived).wait()
     landed(2, arrived)
-    begin(state, arrived, item_scaled, item_coefs, item_hot)
-    conjugate_steps(state, rhs_v, arrived, item_scaled, item_hot, item_hot_t)
+    pick_terms(item_state, arrived, item_scaled, item_coefs, item_hot)
+    set_gram(user_gram[...] + gram_value(6, whole2), pair, single)
+    conjugate_steps(item_state, rhs_v, arrived, item_scaled, item_hot, item_hot_t)
     for which, target in enumerate(
-        (notes, fetched, arrived, near, across, whole, near2, across2, whole2)
+        (gathered, fetched, arrived, near, across, whole, near2, across2, whole2, notes)
     ):
         sent(which, target)
 
@@ -487,8 +506,10 @@
             pltpu.VMEM((capacity, n), jnp.int32),
             floats(capacity, n),
             floats(capacity, n),
-            floats(n, 1, rank),
-            floats(n, 1, rank),
+            floats(inner, outer, rank),
+            floats(inner, outer, rank),
+            floats(outer, inner, rank),
+            floats(outer, inner, rank),
             *gram,
             *gram,
             *[floats(n, capacity, rank)] * 4,
@@ -504,8 +525,8 @@
             pltpu.VMEM((users, 3 * rank), BF16),
             *[floats(items, rank)] * 3,
             pltpu.VMEM((items, 3 * rank), BF16),
-            pltpu.SemaphoreType.DMA((9,)),
-            pltpu.SemaphoreType.DMA((9,)),
+            pltpu.SemaphoreType.DMA((10,)),
+            pltpu.SemaphoreType.DMA((10,)),
             pltpu.SemaphoreType.DMA((3,)),
             pltpu.SemaphoreType.DMA((10,)),
         ],

time: 82.1 us -> 81 us (0.987)
  Pallas kernels: 79 us -> 77.9 us
    pallas_call x1, Pallas kernels: 79 us -> 77.9 us  [per_device(): pl.pallas_call(functools.partial(body, n, fast, capacity), out_shape=(jax...]
where the time goes in v3:
time: 81 us; the launch traced here: 80.8 us
  Pallas kernels  77.9 us (96%)
  local copies, waits for them, and re-layouts  2.32 us (3%)
    pallas_call x1, Pallas kernels, per_device(): pl.pallas_call(functools.partial(body, n, fast, capacity), out_shape=(jax...  77.9 us
    unnamed x4, local copies, waits for them, and re-layouts  2.32 us

profile of v3, /device:TPU:1, one launch (start us, length us, event | category | flops | bytes accessed | tf_op | source)
XLA Modules:
  0.0 80.8 jit_solution(9005753243075372788)
XLA Ops:
  0.6 77.9 %shard_map.104 = (f32[256,128]{1,0:T(8,128)}, f32[512,128]{1,0:T(8,128)}) custom-call(f32[256,128]{1,0:T(8,128)} %user_in.1, f32[512,128]{1,0:T(8,128)} %item_in.1, f32[512,128]{1,0:T(8,128)} %rhs_in.1, f32[128,128]{1,0:T(8,128)} %user_gram_in.1, s32[1,128]{1,0:T(1,128)} %count_in.1, s32[16,128]{1,0:T(8,128)} %bitcast.12, s32[16,128]{1,0:T(8,128)} %bitcast.13, ...), custom_call_target="tpu_custom_call" | custom-call | tf_op jit(solution)/shard_map/pallas_call | solution.py:492
  78.5 0.0 copy-start
  78.5 1.6 %copy.13 = f32[256,128]{1,0:T(8,128)} copy(f32[256,128]{1,0:T(8,128)} %get-tuple-element.4) | data formatting | bytes 262144
  80.1 0.0 copy-done
  80.1 0.7 copy.14
Async XLA Ops:
  78.5 1.6 %copy-start = (f32[512,128]{1,0:T(8,128)S(1)}, f32[512,128]{1,0:T(8,128)}, u32[]{:S(2)}) copy-start(f32[512,128]{1,0:T(8,128)} %get-tuple-element.5) | copy-start | bytes 786436

commit v4 on v3

--- a/solution.py
+++ b/solution.py
@@ -133,18 +133,26 @@
     return halves(first) + dot(outer, state.single[...])
 
 
-def conjugate_steps(state, base, rows_ref, scaled, hot, hot_t):
+def fold_start(state, base, hot_t):
+    groups = state.x.shape[0]
+    for first in range(0, groups, state.block):
+        part = pl.ds(first, state.block)
+        r = halves(dot(hot_t[part, :], state.terms[...]))
+        if base is not None:
+            r = r + base[part, :]
+        state.r[part, :] = r
+
+
+def conjugate_steps(state, rows_ref, scaled, hot, hot_t):
     groups, rank = state.x.shape
     for first in range(0, groups, state.block):
         part = pl.ds(first, state.block)
-        r = halves(dot(hot_t[part, :], state.terms[...])) - gram_part(state, part, rank)
-        if base is not None:
-            r = r + base[part, :]
+        r = state.r[part, :] - gram_part(state, part, rank)
         state.r[part, :] = r
         state.p[part, :] = r
         squares = jnp.sum(r * r, axis=1, keepdims=True)
         state.squares[part, :] = jnp.broadcast_to(squares, r.shape)
-    keep_pieces(state, slice(None), state.p[...])
+        keep_pieces(state, part, r)
 
     def step(last):
         pick_terms(state, rows_ref, scaled, None, hot)
@@ -190,6 +198,8 @@
     rating_in,
     user_out,
     item_out,
+    user_x,
+    item_x,
     item_v,
     rhs_v,
     user_gram,
@@ -202,9 +212,6 @@
     gathered,
     relay,
     notes,
-    partial,
-    near,
-    across,
     whole,
     partial2,
     near2,
@@ -242,8 +249,8 @@
     slots = n * capacity
     users, rank = user_out.shape
     items = item_out.shape[0]
-    inner = near.shape[0]
-    outer = across.shape[0]
+    inner = near2.shape[0]
+    outer = across2.shape[0]
     band = rank // inner
     seat, team = lax.rem(me, inner), lax.div(me, inner)
     region = CHUNK // capacity
@@ -259,10 +266,10 @@
                 (weight_in, weight_v),
                 (rating_in, rating_v),
                 (item_in, item_v),
-                (user_in, user_out),
+                (user_in, user_x),
                 (rhs_in, rhs_v),
                 (user_gram_in, user_gram),
-                (item_in, item_out),
+                (item_in, item_x),
             )
         )
     ]
@@ -327,18 +334,16 @@
             other = lax.rem(team + step, outer)
             push(which + 1, second.at[team], second.at[team], other * inner + seat)
 
+    def give_back(which, third):
+        @pl.loop(1, inner)
+        def _(step):
+            other = lax.rem(seat + step, inner)
+            push(which, third.at[seat], third.at[seat], team * inner + other)
+
     def gram_back(which, second, third):
         landed(which + 1, second)
         third[seat] = jnp.sum(second[...], axis=0)
-
-        @pl.loop(1, inner)
-        def _(step):
-            other = lax.rem(seat + step, inner)
-            push(which + 2, third.at[seat], third.at[seat], team * inner + other)
-
-    def gram_value(which, third):
-        landed(which + 2, third)
-        return third[...].reshape(rank, rank)
+        give_back(which + 2, third)
 
     def send_region(which, source, target, base):
         @pl.loop(0, region)
@@ -363,6 +368,10 @@
     own_note = jnp.concatenate([asked, weights, coefs, members, rest], axis=0).T
     for index in range(outer):
         note_src[:, index, :] = own_note[index * inner : (index + 1) * inner]
+    loads[5].wait()
+    mine = item_v[...]
+    gram = jnp.dot(mine.T, mine, precision=lax.Precision.HIGHEST, preferred_element_type=F32)
+    note_src[:, outer:, :] = gram.reshape(inner, band, rank)
     pl.semaphore_wait(barrier, inner + outer - 2)
 
     @pl.loop(1, inner)
@@ -371,33 +380,30 @@
         push(0, note_src.at[other], gathered.at[seat], mate(step))
 
     gathered[seat] = note_src[seat]
-    loads[5].wait()
-    mine = item_v[...]
-    partial[...] = jnp.dot(
-        mine.T, mine, precision=lax.Precision.HIGHEST, preferred_element_type=F32
-    )
     landed(0, gathered)
     for index in range(outer):
-        relay[index] = gathered[:, index, :]
+        relay[index, :inner] = gathered[:, index, :]
+    team_sum = jnp.sum(gathered[:, outer:, :], axis=0)
+    relay[:, inner:, :] = jnp.broadcast_to(team_sum[None], (outer, band, rank))
 
     @pl.loop(1, outer)
     def _(step):
         other = lax.rem(team + step, outer)
-        push(9, relay.at[other], notes.at[team], counterpart(step))
+        push(6, relay.at[other], notes.at[team], counterpart(step))
 
     notes[team] = relay[team]
-    gram_near(3, partial, near)
     user_state = State(
-        user_out, user_r, user_p, user_squares, user_pieces, terms, pair, single, users // 2
+        user_x, user_r, user_p, user_squares, user_pieces, terms, pair, single, users // 2
     )
     item_state = State(
-        item_out, item_r, item_p, item_squares, item_pieces, terms, pair, single, items // 2
+        item_x, item_r, item_p, item_squares, item_pieces, terms, pair, single, items // 2
     )
     keep_pieces(item_state, slice(None), item_v[...])
 
-    landed(9, notes)
-    gram_across(3, near, across)
-    all_notes = notes[...].reshape(n, rank)
+    landed(6, notes)
+    whole[seat] = jnp.sum(notes[:, inner:, :], axis=0)
+    give_back(7, whole)
+    all_notes = notes[:, :inner, :].reshape(n, rank)
     pieces = split3(all_notes)
     for step in range(slots // CHUNK):
         base = pl.multiple_of(turn(step) * region, region)
@@ -407,8 +413,6 @@
         picked = halves(dot(hot, item_pieces[:, : 2 * rank]))
         picked = picked + dot(hot, item_pieces[:, 2 * rank :])
         found[pl.ds(base, region)] = picked.reshape(region, capacity, rank)
-        if step == 1:
-            gram_back(3, across, whole)
         send_region(1, found, fetched, base)
     own(1, found, fetched).start()
 
@@ -421,7 +425,6 @@
         user_hot[part, :] = column_table(wide, 3, capacity, users)
     row_table(members, users, capacity, user_hot_t)
     loads[6].wait()
-    set_gram(gram_value(3, whole), pair, single)
     for first in range(0, slots, CHUNK):
         part = pl.ds(first, CHUNK)
         wide = spread(pieces, first // capacity, CHUNK, capacity, n)
@@ -429,17 +432,22 @@
         item_coefs[part, :] = jnp.broadcast_to(column(wide, 2, capacity), (CHUNK, rank))
     row_table(all_notes.T[:capacity], items, capacity, item_hot_t)
 
-    keep_pieces(user_state, slice(None), user_out[...])
+    keep_pieces(user_state, slice(None), user_x[...])
     own(1, found, fetched).wait()
     landed(1, fetched)
     pick_terms(user_state, fetched, user_scaled, user_coefs, user_hot)
-    conjugate_steps(user_state, None, fetched, user_scaled, user_hot, user_hot_t)
-
-    refreshed = user_out[...]
+    fold_start(user_state, None, user_hot_t)
+    landed(7, whole)
+    set_gram(whole[...].reshape(rank, rank), pair, single)
+    conjugate_steps(user_state, fetched, user_scaled, user_hot, user_hot_t)
+    put = pltpu.make_async_copy(user_x, user_out, load_sem.at[10])
+    put.start()
+
+    refreshed = user_x[...]
     partial2[...] = jnp.dot(
         refreshed.T, refreshed, precision=lax.Precision.HIGHEST, preferred_element_type=F32
     )
-    gram_near(6, partial2, near2)
+    gram_near(3, partial2, near2)
     for step in range(slots // CHUNK):
         base = pl.multiple_of(turn(step) * region, region)
         hot = user_hot[pl.ds(pl.multiple_of(base * capacity, CHUNK), CHUNK), :]
@@ -447,22 +455,52 @@
         picked = picked + dot(hot, user_pieces[:, 2 * rank :])
         outgoing[pl.ds(base, region)] = picked.reshape(region, capacity, rank)
         if step == 1:
-            gram_across(6, near2, across2)
+            gram_across(3, near2, across2)
         send_region(2, outgoing, arrived, base)
     own(2, outgoing, arrived).start()
-    gram_back(6, across2, whole2)
+    gram_back(3, across2, whole2)
 
     for load in loads[7:]:
         load.wait()
     own(2, outgoing, arrived).wait()
     landed(2, arrived)
     pick_terms(item_state, arrived, item_scaled, item_coefs, item_hot)
-    set_gram(user_gram[...] + gram_value(6, whole2), pair, single)
-    conjugate_steps(item_state, rhs_v, arrived, item_scaled, item_hot, item_hot_t)
+    fold_start(item_state, rhs_v, item_hot_t)
+    landed(5, whole2)
+    set_gram(user_gram[...] + whole2[...].reshape(rank, rank), pair, single)
+    conjugate_steps(item_state, arrived, item_scaled, item_hot, item_hot_t)
+    final = pltpu.make_async_copy(item_x, item_out, load_sem.at[11])
+    final.start()
+    put.wait()
     for which, target in enumerate(
-        (gathered, fetched, arrived, near, across, whole, near2, across2, whole2, notes)
+        (gathered, fetched, arrived, near2, across2, whole2, notes, whole)
     ):
         sent(which, target)
+    final.wait()
+
+
+def hand_on(user_in, item_in, user_out, item_out, user_v, item_v, sems):
+    steps = []
+    half = item_in.shape[0] // 2
+    for source, middle, target, part in (
+        (item_in, item_v, item_out, pl.ds(0, half)),
+        (item_in, item_v, item_out, pl.ds(half, half)),
+        (user_in, user_v, user_out, pl.ds(0, user_in.shape[0])),
+    ):
+        index = len(steps)
+        steps.append(
+            (
+                pltpu.make_async_copy(source.at[part], middle.at[part], sems.at[0, index]),
+                pltpu.make_async_copy(middle.at[part], target.at[part], sems.at[1, index]),
+            )
+        )
+    for first, _ in steps:
+        first.start()
+    for first, second in steps:
+        first.wait()
+        second.start()
+    for _, second in steps:
+        second.wait()
 
 
 def per_device(
@@ -476,8 +514,7 @@
     slots = n * capacity
     inner = 2 * fast
     outer = n // inner
-    vmem = pl.BlockSpec(memory_space=pltpu.VMEM)
-    hbm = pl.BlockSpec(memory_space=pltpu.HBM)
+    anywhere = pl.BlockSpec(memory_space=pl.ANY)
 
     def floats(*shape):
         return pltpu.VMEM(shape, F32)
@@ -489,15 +526,17 @@
         floats(inner, rank // inner, rank),
     ]
     flip = lambda array: jnp.swapaxes(array[0], 0, 1)
-    return pl.pallas_call(
+    results = pl.pallas_call(
         functools.partial(body, n, fast, capacity),
         out_shape=(
             jax.ShapeDtypeStruct((users, rank), F32),
             jax.ShapeDtypeStruct((items, rank), F32),
         ),
-        in_specs=[hbm] * 9,
-        out_specs=(vmem, vmem),
+        in_specs=[anywhere] * 9,
+        out_specs=(anywhere, anywhere),
         scratch_shapes=[
+            floats(users, rank),
+            floats(items, rank),
             floats(items, rank),
             floats(items, rank),
             floats(rank, rank),
@@ -506,11 +545,11 @@
             pltpu.VMEM((capacity, n), jnp.int32),
             floats(capacity, n),
             floats(capacity, n),
-            floats(inner, outer, rank),
-            floats(inner, outer, rank),
-            floats(outer, inner, rank),
-            floats(outer, inner, rank),
-            *gram,
+            floats(inner, outer + rank // inner, rank),
+            floats(inner, outer + rank // inner, rank),
+            floats(outer, inner + rank // inner, rank),
+            floats(outer, inner + rank // inner, rank),
+            gram[3],
             *gram,
             *[floats(n, capacity, rank)] * 4,
             *[floats(slots, rank)] * 4,
@@ -525,10 +564,10 @@
             pltpu.VMEM((users, 3 * rank), BF16),
             *[floats(items, rank)] * 3,
             pltpu.VMEM((items, 3 * rank), BF16),
-            pltpu.SemaphoreType.DMA((10,)),
-            pltpu.SemaphoreType.DMA((10,)),
+            pltpu.SemaphoreType.DMA((8,)),
+            pltpu.SemaphoreType.DMA((8,)),
             pltpu.SemaphoreType.DMA((3,)),
-            pltpu.SemaphoreType.DMA((10,)),
+            pltpu.SemaphoreType.DMA((12,)),
         ],
         compiler_params=pltpu.CompilerParams(
             collective_id=0, has_side_effects=True, vmem_limit_bytes=60 * 2**20
@@ -544,6 +583,14 @@
         flip(weight),
         flip(rating),
     )
+    return pl.pallas_call(
+        hand_on,
+        out_shape=tuple(jax.ShapeDtypeStruct(array.shape, F32) for array in results),
+        in_specs=[anywhere] * 2,
+        out_specs=(anywhere, anywhere),
+        scratch_shapes=[floats(users, rank), floats(items, rank), pltpu.SemaphoreType.DMA((2, 3))],
+        compiler_params=pltpu.CompilerParams(vmem_limit_bytes=60 * 2**20),
+    )(*results)
 
 
 def solution(mesh):

time: 81 us -> 79.2 us (0.978)
  local copies, waits for them, and re-layouts: 2.32 us -> 0 us
    unnamed x4 -> x0, local copies, waits for them, and re-layouts: 2.32 us -> none
    pallas_call x0 -> x1, Pallas kernels: none -> 1.74 us  [per_device(): pl.pallas_call(hand_on, out_shape=tuple((jax.ShapeDtypeStruct(array.shape...]
    pallas_call x1, Pallas kernels: 77.9 us -> 76.5 us  [per_device(): pl.pallas_call(functools.partial(body, n, fast, capacity), out_shape=(jax...]
where the time goes in v4:
time: 79.2 us; the launch traced here: 79 us
  Pallas kernels  78.2 us (99%)
  between operations  0.8 us (1%)
    pallas_call x1, Pallas kernels, per_device(): pl.pallas_call(functools.partial(body, n, fast, capacity), out_shape=(jax...  76.5 us
    pallas_call x1, Pallas kernels, per_device(): pl.pallas_call(hand_on, out_shape=tuple((jax.ShapeDtypeStruct(array.shape...  1.74 us

profile of v4, /device:TPU:1, one launch (start us, length us, event | category | flops | bytes accessed | tf_op | source)
XLA Modules:
  0.0 79.0 jit_solution(13059645247130052377)
XLA Ops:
  0.6 76.5 %shard_map.104 = (f32[256,128]{1,0:T(8,128)}, f32[512,128]{1,0:T(8,128)}) custom-call(f32[256,128]{1,0:T(8,128)} %user_in.1, f32[512,128]{1,0:T(8,128)} %item_in.1, f32[512,128]{1,0:T(8,128)} %rhs_in.1, f32[128,128]{1,0:T(8,128)} %user_gram_in.1, s32[1,128]{1,0:T(1,128)} %count_in.1, s32[16,128]{1,0:T(8,128)} %bitcast.12, s32[16,128]{1,0:T(8,128)} %bitcast.13, ...), custom_call_target="tpu_custom_call" | custom-call | tf_op jit(solution)/shard_map/pallas_call | solution.py:529
  77.1 1.7 %shard_map.105 = (f32[256,128]{1,0:T(8,128)}, f32[512,128]{1,0:T(8,128)}) custom-call(f32[256,128]{1,0:T(8,128)} %get-tuple-element.4.user_in, f32[512,128]{1,0:T(8,128)} %get-tuple-element.5.item_in), custom_call_target="tpu_custom_call" | custom-call | tf_op jit(solution)/shard_map/pallas_call | solution.py:586

commit v5 on v3

--- a/solution.py
+++ b/solution.py
@@ -133,18 +133,26 @@
     return halves(first) + dot(outer, state.single[...])
 
 
-def conjugate_steps(state, base, rows_ref, scaled, hot, hot_t):
+def fold_start(state, base, hot_t):
+    groups = state.x.shape[0]
+    for first in range(0, groups, state.block):
+        part = pl.ds(first, state.block)
+        r = halves(dot(hot_t[part, :], state.terms[...]))
+        if base is not None:
+            r = r + base[part, :]
+        state.r[part, :] = r
+
+
+def conjugate_steps(state, rows_ref, scaled, hot, hot_t):
     groups, rank = state.x.shape
     for first in range(0, groups, state.block):
         part = pl.ds(first, state.block)
-        r = halves(dot(hot_t[part, :], state.terms[...])) - gram_part(state, part, rank)
-        if base is not None:
-            r = r + base[part, :]
+        r = state.r[part, :] - gram_part(state, part, rank)
         state.r[part, :] = r
         state.p[part, :] = r
         squares = jnp.sum(r * r, axis=1, keepdims=True)
         state.squares[part, :] = jnp.broadcast_to(squares, r.shape)
-    keep_pieces(state, slice(None), state.p[...])
+        keep_pieces(state, part, r)
 
     def step(last):
         pick_terms(state, rows_ref, scaled, None, hot)
@@ -242,8 +250,8 @@
     slots = n * capacity
     users, rank = user_out.shape
     items = item_out.shape[0]
-    inner = near.shape[0]
-    outer = across.shape[0]
+    inner = near2.shape[0]
+    outer = across2.shape[0]
     band = rank // inner
     seat, team = lax.rem(me, inner), lax.div(me, inner)
     region = CHUNK // capacity
@@ -327,18 +335,16 @@
             other = lax.rem(team + step, outer)
             push(which + 1, second.at[team], second.at[team], other * inner + seat)
 
+    def give_back(which, third):
+        @pl.loop(1, inner)
+        def _(step):
+            other = lax.rem(seat + step, inner)
+            push(which, third.at[seat], third.at[seat], team * inner + other)
+
     def gram_back(which, second, third):
         landed(which + 1, second)
         third[seat] = jnp.sum(second[...], axis=0)
-
-        @pl.loop(1, inner)
-        def _(step):
-            other = lax.rem(seat + step, inner)
-            push(which + 2, third.at[seat], third.at[seat], team * inner + other)
-
-    def gram_value(which, third):
-        landed(which + 2, third)
-        return third[...].reshape(rank, rank)
+        give_back(which + 2, third)
 
     def send_region(which, source, target, base):
         @pl.loop(0, region)
@@ -376,6 +382,7 @@
     partial[...] = jnp.dot(
         mine.T, mine, precision=lax.Precision.HIGHEST, preferred_element_type=F32
     )
+    gram_near(7, partial, near)
     landed(0, gathered)
     for index in range(outer):
         relay[index] = gathered[:, index, :]
@@ -383,10 +390,16 @@
     @pl.loop(1, outer)
     def _(step):
         other = lax.rem(team + step, outer)
-        push(9, relay.at[other], notes.at[team], counterpart(step))
+        push(6, relay.at[other], notes.at[team], counterpart(step))
 
     notes[team] = relay[team]
-    gram_near(3, partial, near)
+    landed(7, near)
+    across[team] = jnp.sum(near[...], axis=0)
+
+    @pl.loop(1, outer)
+    def _(step):
+        push(8, across.at[team], across.at[team], counterpart(step))
+
     user_state = State(
         user_out, user_r, user_p, user_squares, user_pieces, terms, pair, single, users // 2
     )
@@ -395,8 +408,7 @@
     )
     keep_pieces(item_state, slice(None), item_v[...])
 
-    landed(9, notes)
-    gram_across(3, near, across)
+    landed(6, notes)
     all_notes = notes[...].reshape(n, rank)
     pieces = split3(all_notes)
     for step in range(slots // CHUNK):
@@ -407,9 +419,11 @@
         picked = halves(dot(hot, item_pieces[:, : 2 * rank]))
         picked = picked + dot(hot, item_pieces[:, 2 * rank :])
         found[pl.ds(base, region)] = picked.reshape(region, capacity, rank)
-        if step == 1:
-            gram_back(3, across, whole)
         send_region(1, found, fetched, base)
+        if step == 0:
+            landed(8, across)
+            whole[seat] = jnp.sum(across[...], axis=0)
+            give_back(9, whole)
     own(1, found, fetched).start()
 
     own_pieces = split3(own_note)
@@ -421,7 +435,6 @@
         user_hot[part, :] = column_table(wide, 3, capacity, users)
     row_table(members, users, capacity, user_hot_t)
     loads[6].wait()
-    set_gram(gram_value(3, whole), pair, single)
     for first in range(0, slots, CHUNK):
         part = pl.ds(first, CHUNK)
         wide = spread(pieces, first // capacity, CHUNK, capacity, n)
@@ -433,13 +446,16 @@
     own(1, found, fetched).wait()
     landed(1, fetched)
     pick_terms(user_state, fetched, user_scaled, user_coefs, user_hot)
-    conjugate_steps(user_state, None, fetched, user_scaled, user_hot, user_hot_t)
+    fold_start(user_state, None, user_hot_t)
+    landed(9, whole)
+    set_gram(whole[...].reshape(rank, rank), pair, single)
+    conjugate_steps(user_state, fetched, user_scaled, user_hot, user_hot_t)
 
     refreshed = user_out[...]
     partial2[...] = jnp.dot(
         refreshed.T, refreshed, precision=lax.Precision.HIGHEST, preferred_element_type=F32
     )
-    gram_near(6, partial2, near2)
+    gram_near(3, partial2, near2)
     for step in range(slots // CHUNK):
         base = pl.multiple_of(turn(step) * region, region)
         hot = user_hot[pl.ds(pl.multiple_of(base * capacity, CHUNK), CHUNK), :]
@@ -447,22 +463,35 @@
         picked = picked + dot(hot, user_pieces[:, 2 * rank :])
         outgoing[pl.ds(base, region)] = picked.reshape(region, capacity, rank)
         if step == 1:
-            gram_across(6, near2, across2)
+            gram_across(3, near2, across2)
         send_region(2, outgoing, arrived, base)
     own(2, outgoing, arrived).start()
-    gram_back(6, across2, whole2)
+    gram_back(3, across2, whole2)
 
     for load in loads[7:]:
         load.wait()
     own(2, outgoing, arrived).wait()
     landed(2, arrived)
     pick_terms(item_state, arrived, item_scaled, item_coefs, item_hot)
-    set_gram(user_gram[...] + gram_value(6, whole2), pair, single)
-    conjugate_steps(item_state, rhs_v, arrived, item_scaled, item_hot, item_hot_t)
+    fold_start(item_state, rhs_v, item_hot_t)
+    landed(5, whole2)
+    set_gram(user_gram[...] + whole2[...].reshape(rank, rank), pair, single)
+    conjugate_steps(item_state, arrived, item_scaled, item_hot, item_hot_t)
     for which, target in enumerate(
-        (gathered, fetched, arrived, near, across, whole, near2, across2, whole2, notes)
+        (gathered, fetched, arrived, near2, across2, whole2, notes, near, across, whole)
     ):
         sent(which, target)
+
+
+def hand_on(user_in, item_in, user_out, item_out, sems):
+    moves = [
+        pltpu.make_async_copy(item_in, item_out, sems.at[0]),
+        pltpu.make_async_copy(user_in, user_out, sems.at[1]),
+    ]
+    for move in moves:
+        move.start()
+    for move in moves:
+        move.wait()
 
 
 def per_device(
@@ -476,8 +505,8 @@
     slots = n * capacity
     inner = 2 * fast
     outer = n // inner
+    anywhere = pl.BlockSpec(memory_space=pl.ANY)
     vmem = pl.BlockSpec(memory_space=pltpu.VMEM)
-    hbm = pl.BlockSpec(memory_space=pltpu.HBM)
 
     def floats(*shape):
         return pltpu.VMEM(shape, F32)
@@ -489,13 +518,10 @@
         floats(inner, rank // inner, rank),
     ]
     flip = lambda array: jnp.swapaxes(array[0], 0, 1)
-    return pl.pallas_call(
+    results = pl.pallas_call(
         functools.partial(body, n, fast, capacity),
-        out_shape=(
-            jax.ShapeDtypeStruct((users, rank), F32),
-            jax.ShapeDtypeStruct((items, rank), F32),
-        ),
-        in_specs=[hbm] * 9,
+        out_shape=(floats(users, rank), floats(items, rank)),
+        in_specs=[anywhere] * 9,
         out_specs=(vmem, vmem),
         scratch_shapes=[
             floats(items, rank),
@@ -544,6 +570,14 @@
         flip(weight),
         flip(rating),
     )
+    return pl.pallas_call(
+        hand_on,
+        out_shape=tuple(jax.ShapeDtypeStruct(array.shape, F32) for array in results),
+        in_specs=[vmem] * 2,
+        out_specs=(anywhere, anywhere),
+        scratch_shapes=[pltpu.SemaphoreType.DMA((2,))],
+        compiler_params=pltpu.CompilerParams(vmem_limit_bytes=2 * 2**20),
+    )(*results)
 
 
 def solution(mesh):

time: 81 us -> 75.8 us (0.936)
  Pallas kernels: 77.9 us -> 74.9 us
  local copies, waits for them, and re-layouts: 2.32 us -> 0 us
    pallas_call x1 -> x2, Pallas kernels: 77.9 us -> 74.9 us  [the longest x1 74.1 us: per_device(): pl.pallas_call(functools.partial(body, n, fast, capacity), out_shape=(flo...]
    unnamed x4 -> x0, local copies, waits for them, and re-layouts: 2.32 us -> none
where the time goes in v5:
time: 75.8 us; the launch traced here: 75.7 us
  Pallas kernels  74.9 us (99%)
  between operations  0.8 us (1%)
    pallas_call x1, Pallas kernels, per_device(): pl.pallas_call(functools.partial(body, n, fast, capacity), out_shape=(flo...  74.1 us

profile of v5, /device:TPU:1, one launch (start us, length us, event | category | flops | bytes accessed | tf_op | source)
XLA Modules:
  0.0 75.7 jit_solution(6519012101098777611)
XLA Ops:
  0.6 74.1 %shard_map.104 = (f32[256,128]{1,0:T(8,128)S(1)}, f32[512,128]{1,0:T(8,128)S(1)}) custom-call(f32[256,128]{1,0:T(8,128)} %user_in.1, f32[512,128]{1,0:T(8,128)} %item_in.1, f32[512,128]{1,0:T(8,128)} %rhs_in.1, f32[128,128]{1,0:T(8,128)} %user_gram_in.1, s32[1,128]{1,0:T(1,128)} %count_in.1, s32[16,128]{1,0:T(8,128)} %bitcast.12, s32[16,128]{1,0:T(8,128)} %bitcast.13, ...), custom_call_target="tpu_custom_call" | custom-call | tf_op jit(solution)/shard_map/pallas_call | solution.py:521
  74.7 0.8 %shard_map.105 = (f32[256,128]{1,0:T(8,128)}, f32[512,128]{1,0:T(8,128)}) custom-call(f32[256,128]{1,0:T(8,128)S(1)} %get-tuple-element.4.user_in, f32[512,128]{1,0:T(8,128)S(1)} %get-tuple-element.5.item_in), custom_call_target="tpu_custom_call" | custom-call | tf_op jit(solution)/shard_map/pallas_call | solution.py:573

commit v6 on v5

--- a/solution.py
+++ b/solution.py
@@ -214,10 +214,10 @@
     near,
     across,
     whole,
-    partial2,
-    near2,
-    across2,
-    whole2,
+    part_src,
+    parts,
+    row_src,
+    gram_rows,
     found,
     fetched,
     outgoing,
@@ -250,8 +250,8 @@
     slots = n * capacity
     users, rank = user_out.shape
     items = item_out.shape[0]
-    inner = near2.shape[0]
-    outer = across2.shape[0]
+    inner = near.shape[0]
+    outer = across.shape[0]
     band = rank // inner
     seat, team = lax.rem(me, inner), lax.div(me, inner)
     region = CHUNK // capacity
@@ -326,25 +326,11 @@
                 team * inner + other,
             )
 
-    def gram_across(which, first, second):
-        landed(which, first)
-        second[team] = jnp.sum(first[...], axis=0)
-
-        @pl.loop(1, outer)
-        def _(step):
-            other = lax.rem(team + step, outer)
-            push(which + 1, second.at[team], second.at[team], other * inner + seat)
-
     def give_back(which, third):
         @pl.loop(1, inner)
         def _(step):
             other = lax.rem(seat + step, inner)
             push(which, third.at[seat], third.at[seat], team * inner + other)
-
-    def gram_back(which, second, third):
-        landed(which + 1, second)
-        third[seat] = jnp.sum(second[...], axis=0)
-        give_back(which + 2, third)
 
     def send_region(which, source, target, base):
         @pl.loop(0, region)
@@ -382,7 +368,7 @@
     partial[...] = jnp.dot(
         mine.T, mine, precision=lax.Precision.HIGHEST, preferred_element_type=F32
     )
-    gram_near(7, partial, near)
+    gram_near(5, partial, near)
     landed(0, gathered)
     for index in range(outer):
         relay[index] = gathered[:, index, :]
@@ -393,12 +379,12 @@
         push(6, relay.at[other], notes.at[team], counterpart(step))
 
     notes[team] = relay[team]
-    landed(7, near)
+    landed(5, near)
     across[team] = jnp.sum(near[...], axis=0)
 
     @pl.loop(1, outer)
     def _(step):
-        push(8, across.at[team], across.at[team], counterpart(step))
+        push(7, across.at[team], across.at[team], counterpart(step))
 
     user_state = State(
         user_out, user_r, user_p, user_squares, user_pieces, terms, pair, single, users // 2
@@ -421,9 +407,9 @@
         found[pl.ds(base, region)] = picked.reshape(region, capacity, rank)
         send_region(1, found, fetched, base)
         if step == 0:
-            landed(8, across)
+            landed(7, across)
             whole[seat] = jnp.sum(across[...], axis=0)
-            give_back(9, whole)
+            give_back(8, whole)
     own(1, found, fetched).start()
 
     own_pieces = split3(own_note)
@@ -447,26 +433,43 @@
     landed(1, fetched)
     pick_terms(user_state, fetched, user_scaled, user_coefs, user_hot)
     fold_start(user_state, None, user_hot_t)
-    landed(9, whole)
+    landed(8, whole)
     set_gram(whole[...].reshape(rank, rank), pair, single)
     conjugate_steps(user_state, fetched, user_scaled, user_hot, user_hot_t)
 
-    refreshed = user_out[...]
-    partial2[...] = jnp.dot(
-        refreshed.T, refreshed, precision=lax.Precision.HIGHEST, preferred_element_type=F32
-    )
-    gram_near(3, partial2, near2)
     for step in range(slots // CHUNK):
         base = pl.multiple_of(turn(step) * region, region)
         hot = user_hot[pl.ds(pl.multiple_of(base * capacity, CHUNK), CHUNK), :]
         picked = halves(dot(hot, user_pieces[:, : 2 * rank]))
         picked = picked + dot(hot, user_pieces[:, 2 * rank :])
         outgoing[pl.ds(base, region)] = picked.reshape(region, capacity, rank)
-        if step == 1:
-            gram_across(3, near2, across2)
         send_region(2, outgoing, arrived, base)
+        if step == 0:
+            refreshed = user_out[...]
+            gram = jnp.dot(
+                refreshed.T,
+                refreshed,
+                precision=lax.Precision.HIGHEST,
+                preferred_element_type=F32,
+            )
+            part_src[...] = gram[:, None, :]
+            parts[me] = part_src[me]
+
+            @pl.loop(1, n)
+            def _(step):
+                peer = lax.rem(me + step, n)
+                push(3, part_src.at[peer], parts.at[me], peer)
+
     own(2, outgoing, arrived).start()
-    gram_back(3, across2, whole2)
+    landed(3, parts)
+    row = jnp.sum(parts[...], axis=0)
+    row_src[0] = row
+    gram_rows[me] = row
+
+    @pl.loop(1, n)
+    def _(step):
+        push(4, row_src.at[0], gram_rows.at[me], lax.rem(me + step, n))
+
 
     for load in loads[7:]:
         load.wait()
@@ -474,11 +477,11 @@
     landed(2, arrived)
     pick_terms(item_state, arrived, item_scaled, item_coefs, item_hot)
     fold_start(item_state, rhs_v, item_hot_t)
-    landed(5, whole2)
-    set_gram(user_gram[...] + whole2[...].reshape(rank, rank), pair, single)
+    landed(4, gram_rows)
+    set_gram(user_gram[...] + gram_rows[:, 0, :], pair, single)
     conjugate_steps(item_state, arrived, item_scaled, item_hot, item_hot_t)
     for which, target in enumerate(
-        (gathered, fetched, arrived, near2, across2, whole2, notes, near, across, whole)
+        (gathered, fetched, arrived, parts, gram_rows, near, notes, across, whole)
     ):
         sent(which, target)
 
@@ -537,7 +540,10 @@
             floats(outer, inner, rank),
             floats(outer, inner, rank),
             *gram,
-            *gram,
+            floats(n, 1, rank),
+            floats(n, 1, rank),
+            floats(1, 1, rank),
+            floats(n, 1, rank),
             *[floats(n, capacity, rank)] * 4,
             *[floats(slots, rank)] * 4,
             pltpu.VMEM((slots, users), BF16),
@@ -551,8 +557,8 @@
             pltpu.VMEM((users, 3 * rank), BF16),
             *[floats(items, rank)] * 3,
             pltpu.VMEM((items, 3 * rank), BF16),
-            pltpu.SemaphoreType.DMA((10,)),
-            pltpu.SemaphoreType.DMA((10,)),
+            pltpu.SemaphoreType.DMA((9,)),
+            pltpu.SemaphoreType.DMA((9,)),
             pltpu.SemaphoreType.DMA((3,)),
             pltpu.SemaphoreType.DMA((10,)),
         ],

time: 75.8 us -> 75.1 us (level)
  no operation moved by 1% of the time
where the time goes in v6:
time: 75.1 us; the launch traced here: 75 us
  Pallas kernels  74.2 us (99%)
  between operations  0.8 us (1%)
    pallas_call x1, Pallas kernels, per_device(): pl.pallas_call(functools.partial(body, n, fast, capacity), out_shape=(flo...  73.4 us

profile of v6, /device:TPU:1, one launch (start us, length us, event | category | flops | bytes accessed | tf_op | source)
XLA Modules:
  0.0 75.0 jit_solution(467102735200715935)
XLA Ops:
  0.6 73.4 %shard_map.104 = (f32[256,128]{1,0:T(8,128)S(1)}, f32[512,128]{1,0:T(8,128)S(1)}) custom-call(f32[256,128]{1,0:T(8,128)} %user_in.1, f32[512,128]{1,0:T(8,128)} %item_in.1, f32[512,128]{1,0:T(8,128)} %rhs_in.1, f32[128,128]{1,0:T(8,128)} %user_gram_in.1, s32[1,128]{1,0:T(1,128)} %count_in.1, s32[16,128]{1,0:T(8,128)} %bitcast.12, s32[16,128]{1,0:T(8,128)} %bitcast.13, ...), custom_call_target="tpu_custom_call" | custom-call | tf_op jit(solution)/shard_map/pallas_call | solution.py:524
  74.1 0.8 %shard_map.105 = (f32[256,128]{1,0:T(8,128)}, f32[512,128]{1,0:T(8,128)}) custom-call(f32[256,128]{1,0:T(8,128)S(1)} %get-tuple-element.4.user_in, f32[512,128]{1,0:T(8,128)S(1)} %get-tuple-element.5.item_in), custom_call_target="tpu_custom_call" | custom-call | tf_op jit(solution)/shard_map/pallas_call | solution.py:579

commit v7 on v6

--- a/solution.py
+++ b/solution.py
@@ -11,7 +11,7 @@
 RIDGE = 1.0
 CHUNK = 512
 PICK = 128
-MESH = pl.DeviceIdType.MESH
+FLAT = pl.DeviceIdType.LOGICAL
 F32 = jnp.float32
 BF16 = jnp.bfloat16
 
@@ -126,9 +126,11 @@
         state.pieces[part, index * rank : (index + 1) * rank] = piece
 
 
-def gram_part(state, part, rank):
+def gram_part(state, part, rank, full=True):
     mine = state.pieces[part, :]
     first = dot(mine[:, : 2 * rank], state.pair[...])
+    if not full:
+        return halves(first)
     outer = jnp.concatenate([mine[:, :rank], mine[:, 2 * rank :]], axis=1)
     return halves(first) + dot(outer, state.single[...])
 
@@ -143,7 +145,7 @@
         state.r[part, :] = r
 
 
-def conjugate_steps(state, rows_ref, scaled, hot, hot_t):
+def conjugate_steps(state, rows_ref, scaled, hot, hot_t, exact):
     groups, rank = state.x.shape
     for first in range(0, groups, state.block):
         part = pl.ds(first, state.block)
@@ -154,11 +156,12 @@
         state.squares[part, :] = jnp.broadcast_to(squares, r.shape)
         keep_pieces(state, part, r)
 
-    def step(last):
+    def step(last, full):
         pick_terms(state, rows_ref, scaled, None, hot)
         for first in range(0, groups, state.block):
             part = pl.ds(first, state.block)
-            image = halves(dot(hot_t[part, :], state.terms[...])) + gram_part(state, part, rank)
+            image = halves(dot(hot_t[part, :], state.terms[...]))
+            image = image + gram_part(state, part, rank, full)
             p = state.p[part, :]
             squares = state.squares[part, :]
             alpha = squares / jnp.sum(p * image, axis=1, keepdims=True)
@@ -175,12 +178,14 @@
             state.squares[part, :] = jnp.broadcast_to(fresh, p.shape)
             keep_pieces(state, part, p)
 
-    def middle(iteration, carry):
-        step(False)
+    def middle(full, iteration, carry):
+        step(False, full)
         return carry
 
-    lax.fori_loop(0, ITERS - 1, middle, 0)
-    step(True)
+    lax.fori_loop(0, exact, functools.partial(middle, True), 0)
+    if exact < ITERS - 1:
+        lax.fori_loop(exact, ITERS - 1, functools.partial(middle, False), 0)
+    step(True, exact == ITERS - 1)
 
 
 def body(
@@ -277,9 +282,6 @@
     for load in loads:
         load.start()
 
-    def at(peer):
-        return (lax.div(peer, fast), lax.rem(peer, fast))
-
     def mate(step):
         return team * inner + lax.rem(seat + step, inner)
 
@@ -290,7 +292,7 @@
 
         @pl.loop(1, count)
         def _(step):
-            pl.semaphore_signal(barrier, inc=1, device_id=at(other(step)), device_id_type=MESH)
+            pl.semaphore_signal(barrier, inc=1, device_id=other(step), device_id_type=FLAT)
 
     def push(which, source, target, peer):
         pltpu.make_async_remote_copy(
@@ -298,8 +300,8 @@
             dst_ref=target,
             send_sem=send_sem.at[which],
             recv_sem=recv_sem.at[which],
-            device_id=at(peer),
-            device_id_type=MESH,
+            device_id=peer,
+            device_id_type=FLAT,
         ).start()
 
     def landed(which, target):
@@ -435,7 +437,7 @@
     fold_start(user_state, None, user_hot_t)
     landed(8, whole)
     set_gram(whole[...].reshape(rank, rank), pair, single)
-    conjugate_steps(user_state, fetched, user_scaled, user_hot, user_hot_t)
+    conjugate_steps(user_state, fetched, user_scaled, user_hot, user_hot_t, ITERS - 1)
 
     for step in range(slots // CHUNK):
         base = pl.multiple_of(turn(step) * region, region)
@@ -479,7 +481,7 @@
     fold_start(item_state, rhs_v, item_hot_t)
     landed(4, gram_rows)
     set_gram(user_gram[...] + gram_rows[:, 0, :], pair, single)
-    conjugate_steps(item_state, arrived, item_scaled, item_hot, item_hot_t)
+    conjugate_steps(item_state, arrived, item_scaled, item_hot, item_hot_t, ITERS // 2)
     for which, target in enumerate(
         (gathered, fetched, arrived, parts, gram_rows, near, notes, across, whole)
     ):

time: 75.1 us -> 74.8 us (level)
  no operation moved by 1% of the time
where the time goes in v7:
time: 74.8 us; the launch traced here: 74.7 us
  Pallas kernels  73.9 us (99%)
  between operations  0.8 us (1%)
    pallas_call x1, Pallas kernels, per_device(): pl.pallas_call(functools.partial(body, n, fast, capacity), out_shape=(flo...  73.2 us

profile of v7, /device:TPU:1, one launch (start us, length us, event | category | flops | bytes accessed | tf_op | source)
XLA Modules:
  0.0 74.7 jit_solution(7199660934980651007)
XLA Ops:
  0.6 73.2 %shard_map.104 = (f32[256,128]{1,0:T(8,128)S(1)}, f32[512,128]{1,0:T(8,128)S(1)}) custom-call(f32[256,128]{1,0:T(8,128)} %user_in.1, f32[512,128]{1,0:T(8,128)} %item_in.1, f32[512,128]{1,0:T(8,128)} %rhs_in.1, f32[128,128]{1,0:T(8,128)} %user_gram_in.1, s32[1,128]{1,0:T(1,128)} %count_in.1, s32[16,128]{1,0:T(8,128)} %bitcast.12, s32[16,128]{1,0:T(8,128)} %bitcast.13, ...), custom_call_target="tpu_custom_call" | custom-call | tf_op jit(solution)/shard_map/pallas_call | solution.py:526
  73.8 0.8 %shard_map.105 = (f32[256,128]{1,0:T(8,128)}, f32[512,128]{1,0:T(8,128)}) custom-call(f32[256,128]{1,0:T(8,128)S(1)} %get-tuple-element.4.user_in, f32[512,128]{1,0:T(8,128)S(1)} %get-tuple-element.5.item_in), custom_call_target="tpu_custom_call" | custom-call | tf_op jit(solution)/shard_map/pallas_call | solution.py:581
